TPU v7x, 32 devices: a whole 2x2x4 slice. The times are simulated.
32 devices in a mesh: tm: 16 (over z, y, core), lat: 2 (over x).
Axes of the slice: x: 2, y: 2, z: 4, core: 2. Of those that a mesh axis runs over, the one named last changes fastest.
Arguments:
- fields: bfloat16 [32, 720, 1440], P('tm', 'lat'), may hold values from -6 to 6
- legendre: bfloat16 [720, 8192], P('lat'), may hold values from -0.21875 to 0.21875
- order_table: int32 [3, 16384], replicated, may hold values from 0 to 720, as said below
- window_start: int32 [1], replicated, may hold values from 0 to 8192
- ridge: float32 [1], replicated, may hold values from 0.3 to 1
Outputs:
- factored: float32 [8192, 8192], P('tm', 'lat')
Inputs may be any that keep to these rules, and one draw needn't show every extreme that they name: `order_table`: row 0 holds each entry's degree, row 1 its order, which is at most the degree and below 720, row 2 is 0 for a cosine and 1 for a sine part, and is 1 only where the order is positive.
All inputs are finite; a program needn't handle non-finite values.
Results may differ from a plain program's by a relative error of at most 0.0048.
Values may be sent and summed in bfloat16 or wider, within the bound.
No kernel may reach another device: no remote copies, remote signals or barrier semaphores. Data moves between devices by JAX's collectives and lax.ppermute only.
A program may use at most 64 MiB of HBM per device.

v0:
```python
import math

import jax
import jax.numpy as jnp
from jax import lax
from jax.sharding import PartitionSpec as P

LMAX = 720
PANEL = 512


def make_basis(nlon):
    half = nlon // 2
    longitude = jnp.arange(nlon, dtype=jnp.int32)[:, None]
    column = jnp.arange(nlon, dtype=jnp.int32)[None, :]
    freq = column % half
    phase = (freq * longitude % nlon).astype(jnp.float32) * (2.0 * math.pi / nlon)
    return jnp.where(column < half, jnp.cos(phase), jnp.sin(phase)).astype(jnp.bfloat16)


def legendre_contract(spectra, legendre, column):
    kcoef = legendre.shape[1]
    width = kcoef // 8

    def one_part(number):
        start = number * width
        chosen_cols = lax.dynamic_slice_in_dim(column, start, width, 0)
        weights = lax.dynamic_slice_in_dim(legendre, start, width, 1).astype(jnp.float32)
        chosen = jnp.take(spectra, chosen_cols, axis=2)
        return jnp.einsum("tlk,lk->tk", chosen, weights)

    parts_out = lax.map(one_part, jnp.arange(8, dtype=jnp.int32))
    return jnp.transpose(parts_out, (1, 0, 2)).reshape(spectra.shape[0], kcoef)


def gram_dot(left, right):
    return lax.dot_general(
        left, right, (((0,), (0,)), ((), ())), preferred_element_type=jnp.float32
    )


def on_device(fields, legendre, order_table, window_start, ridge):
    times_dev, lat_dev, nlon = fields.shape
    kcoef = legendre.shape[1]
    tm_count = lax.axis_size("tm")
    lat_count = lax.axis_size("lat")
    rows_width = kcoef // tm_count
    cols_width = kcoef // lat_count
    tm_index = lax.axis_index("tm")
    lat_index = lax.axis_index("lat")
    window = lax.dynamic_slice_in_dim(order_table, window_start[0], kcoef, 1)
    degree = window[0]
    column = window[1] + nlon // 2 * window[2]
    ridge_diag = ridge[0] * (
        1.0 + (degree * (degree + 1)).astype(jnp.float32) / float(LMAX * (LMAX + 1))
    )
    dft_basis = make_basis(nlon)
    flat = fields.reshape(times_dev * lat_dev, nlon)
    spectra = (
        jnp.dot(flat, dft_basis, preferred_element_type=jnp.float32) * (1.0 / math.sqrt(nlon))
    ).reshape(times_dev, lat_dev, nlon)
    partial_value = legendre_contract(spectra, legendre, column)
    coeffs = lax.psum(partial_value, "lat").astype(jnp.bfloat16)
    row_block = lax.all_to_all(coeffs, "tm", split_axis=1, concat_axis=0, tiled=True)
    local_cols = lax.dynamic_slice_in_dim(coeffs, lat_index * cols_width, cols_width, 1)
    col_block, panel_coef = (
        lax.all_gather(local_cols, "tm", axis=0, tiled=True),
        lax.all_gather(coeffs[:, :PANEL], "tm", axis=0, tiled=True),
    )
    inverse = 1.0 / col_block.shape[0]
    row_glob = tm_index * rows_width + jnp.arange(rows_width, dtype=jnp.int32)
    col_glob = lat_index * cols_width + jnp.arange(cols_width, dtype=jnp.int32)
    panel_pos = jnp.arange(PANEL, dtype=jnp.int32)
    ridge_rows = lax.dynamic_slice_in_dim(ridge_diag, tm_index * rows_width, rows_width, 0)
    zero = jnp.float32(0.0)
    gram_tile = gram_dot(row_block, col_block) * inverse + jnp.where(
        row_glob[:, None] == col_glob[None, :], ridge_rows[:, None], zero
    )
    panel_gram = gram_dot(panel_coef, panel_coef) * inverse + jnp.diag(ridge_diag[:PANEL])
    factor = jnp.linalg.cholesky(panel_gram)
    row_panel = gram_dot(row_block, panel_coef) * inverse + jnp.where(
        row_glob[:, None] == panel_pos[None, :], ridge_rows[:, None], zero
    )
    panel_rows = jax.scipy.linalg.solve_triangular(factor, row_panel.T, lower=True).T
    solved = jax.scipy.linalg.solve_triangular(factor, panel_coef.astype(jnp.float32).T, lower=True)
    upper = (
        jnp.dot(
            solved, col_block, precision=lax.Precision.HIGHEST, preferred_element_type=jnp.float32
        )
        * inverse
    )
    update = jnp.dot(panel_rows, upper, precision=lax.Precision.HIGHEST)
    upper_rows = lax.dynamic_slice_in_dim(
        upper, jnp.minimum(tm_index * rows_width, PANEL - rows_width), rows_width, 0
    )
    left_part = jnp.pad(panel_rows, ((0, 0), (0, cols_width - PANEL)))
    return jnp.where(
        col_glob[None, :] < PANEL,
        left_part,
        jnp.where(row_glob[:, None] < PANEL, upper_rows, gram_tile - update),
    )


def solution(mesh):
    placed = (P("tm", "lat", None), P("lat", None), P(), P(), P())
    return jax.shard_map(
        on_device, mesh=mesh, in_specs=placed, out_specs=P("tm", "lat"), check_vma=False
    )
```

profile of v0, /device:TPU:1, one launch (start us, length us, event | category | flops | bytes accessed | tf_op | source)
XLA Modules:
  0.0 539.1 jit_solution(10980804932324622157)
XLA Ops:
  0.8 37.4 %select_convert_fusion.6 = bf16[1440,1440]{1,0:T(8,128)(2,1)S(1)} fusion(s32[1440]{0:T(1024)S(1)} %add_select_fusion.1, pred[1440]{0:T(1024)(128)(4,1)S(1)} %iota_compare_fusion.6), kind=kLoop, calls=%fused_computation.13.clone.clone.clone.clone.1 | loop fusion | flops 22809600 | bytes 4154400 | tf_op jit(solution)/shard_map/dot_general | solution.py:60
  43.4 7.9 %copy.17 = f32[2,360,1440]{1,0,2:T(2,128)} copy(f32[2,360,1440]{2,1,0:T(8,128)} %bitcast.111) | data formatting | bytes 8294400 | tf_op jit(solution)/shard_map/while | solution.py:32
  52.7 250.9 %while.11 = (s32[]{:T(128)}, f32[8,2,1024]{2,1,0:T(2,128)S(1)}, s32[8]{0:T(128)S(1)}, bf16[360,8192]{1,0:T(8,128)(2,1)}, s32[8192]{0:T(1024)S(1)}, /*index=5*/f3...) while((s32[]{:T(128)}, f32[8,2,1024]{2,1,0:T(2,128)S(1)}, s32[8]{0:T(128)S(1)}, ...), condition=%wide.region_1.2_spmd, body=%wide.region_0.1_spmd.sunk | while | flops 2588678 | bytes 15542447 | solution.py:32
  54.0 7.1 %gather_fusion = f32[1024,2,360]{2,1,0:T(2,128)S(1)} fusion(f32[2,360,1440]{1,0,2:T(2,128)} %get-tuple-element.189, s32[1024]{0:T(1024)S(1)} %fusion.112), kind=kCustom, calls=%fused_computation.clone.1 | custom fusion | bytes 5902336 | tf_op jit(solution)/shard_map/while/body/eval_jaxpr/jit(_take)/gather | solution.py:29
  66.5 16.3 %fusion.113 = f32[1024,2]{1,0:T(8,128)} fusion(f32[1024,2,360]{2,1,0:T(2,128)S(1)} %gather_fusion, pred[1024]{0:T(1024)(128)(4,1)S(1)} %compare_and_fusion.2, f32[1024,360]{1,0:T(8,128)} %copy.36), kind=kLoop, calls=%fused_computation.4.clone.1 | loop fusion | flops 2209792 | bytes 4432896 | tf_op jit(solution)/shard_map/while
  85.3 7.1 %gather_fusion = f32[1024,2,360]{2,1,0:T(2,128)S(1)} fusion(f32[2,360,1440]{1,0,2:T(2,128)} %get-tuple-element.189, s32[1024]{0:T(1024)S(1)} %fusion.112), kind=kCustom, calls=%fused_computation.clone.1 | custom fusion | bytes 5902336 | tf_op jit(solution)/shard_map/while/body/eval_jaxpr/jit(_take)/gather | solution.py:29
  97.9 16.3 %fusion.113 = f32[1024,2]{1,0:T(8,128)} fusion(f32[1024,2,360]{2,1,0:T(2,128)S(1)} %gather_fusion, pred[1024]{0:T(1024)(128)(4,1)S(1)} %compare_and_fusion.2, f32[1024,360]{1,0:T(8,128)} %copy.36), kind=kLoop, calls=%fused_computation.4.clone.1 | loop fusion | flops 2209792 | bytes 4432896 | tf_op jit(solution)/shard_map/while
  116.7 7.1 %gather_fusion = f32[1024,2,360]{2,1,0:T(2,128)S(1)} fusion(f32[2,360,1440]{1,0,2:T(2,128)} %get-tuple-element.189, s32[1024]{0:T(1024)S(1)} %fusion.112), kind=kCustom, calls=%fused_computation.clone.1 | custom fusion | bytes 5902336 | tf_op jit(solution)/shard_map/while/body/eval_jaxpr/jit(_take)/gather | solution.py:29
  129.2 16.3 %fusion.113 = f32[1024,2]{1,0:T(8,128)} fusion(f32[1024,2,360]{2,1,0:T(2,128)S(1)} %gather_fusion, pred[1024]{0:T(1024)(128)(4,1)S(1)} %compare_and_fusion.2, f32[1024,360]{1,0:T(8,128)} %copy.36), kind=kLoop, calls=%fused_computation.4.clone.1 | loop fusion | flops 2209792 | bytes 4432896 | tf_op jit(solution)/shard_map/while
  160.6 16.3 %fusion.113 = f32[1024,2]{1,0:T(8,128)} fusion(f32[1024,2,360]{2,1,0:T(2,128)S(1)} %gather_fusion, pred[1024]{0:T(1024)(128)(4,1)S(1)} %compare_and_fusion.2, f32[1024,360]{1,0:T(8,128)} %copy.36), kind=kLoop, calls=%fused_computation.4.clone.1 | loop fusion | flops 2209792 | bytes 4432896 | tf_op jit(solution)/shard_map/while
  191.9 16.3 %fusion.113 = f32[1024,2]{1,0:T(8,128)} fusion(f32[1024,2,360]{2,1,0:T(2,128)S(1)} %gather_fusion, pred[1024]{0:T(1024)(128)(4,1)S(1)} %compare_and_fusion.2, f32[1024,360]{1,0:T(8,128)} %copy.36), kind=kLoop, calls=%fused_computation.4.clone.1 | loop fusion | flops 2209792 | bytes 4432896 | tf_op jit(solution)/shard_map/while
  210.7 7.1 %gather_fusion = f32[1024,2,360]{2,1,0:T(2,128)S(1)} fusion(f32[2,360,1440]{1,0,2:T(2,128)} %get-tuple-element.189, s32[1024]{0:T(1024)S(1)} %fusion.112), kind=kCustom, calls=%fused_computation.clone.1 | custom fusion | bytes 5902336 | tf_op jit(solution)/shard_map/while/body/eval_jaxpr/jit(_take)/gather | solution.py:29
  223.3 16.3 %fusion.113 = f32[1024,2]{1,0:T(8,128)} fusion(f32[1024,2,360]{2,1,0:T(2,128)S(1)} %gather_fusion, pred[1024]{0:T(1024)(128)(4,1)S(1)} %compare_and_fusion.2, f32[1024,360]{1,0:T(8,128)} %copy.36), kind=kLoop, calls=%fused_computation.4.clone.1 | loop fusion | flops 2209792 | bytes 4432896 | tf_op jit(solution)/shard_map/while
  242.1 7.1 %gather_fusion = f32[1024,2,360]{2,1,0:T(2,128)S(1)} fusion(f32[2,360,1440]{1,0,2:T(2,128)} %get-tuple-element.189, s32[1024]{0:T(1024)S(1)} %fusion.112), kind=kCustom, calls=%fused_computation.clone.1 | custom fusion | bytes 5902336 | tf_op jit(solution)/shard_map/while/body/eval_jaxpr/jit(_take)/gather | solution.py:29
  254.7 16.3 %fusion.113 = f32[1024,2]{1,0:T(8,128)} fusion(f32[1024,2,360]{2,1,0:T(2,128)S(1)} %gather_fusion, pred[1024]{0:T(1024)(128)(4,1)S(1)} %compare_and_fusion.2, f32[1024,360]{1,0:T(8,128)} %copy.36), kind=kLoop, calls=%fused_computation.4.clone.1 | loop fusion | flops 2209792 | bytes 4432896 | tf_op jit(solution)/shard_map/while
  286.0 16.3 %fusion.113 = f32[1024,2]{1,0:T(8,128)} fusion(f32[1024,2,360]{2,1,0:T(2,128)S(1)} %gather_fusion, pred[1024]{0:T(1024)(128)(4,1)S(1)} %compare_and_fusion.2, f32[1024,360]{1,0:T(8,128)} %copy.36), kind=kLoop, calls=%fused_computation.4.clone.1 | loop fusion | flops 2209792 | bytes 4432896 | tf_op jit(solution)/shard_map/while
  303.6 8.2 %psum.7 = bf16[2,8192]{1,0:T(2,128)(2,1)} all-reduce(f32[2,8192]{1,0:T(2,128)S(1)} %bitcast.116), channel_id=1, replica_groups=mesh['tm'=16,'lat'=2] {'lat'}, use_global_device_ids=true, to_apply=%region_2.3 | all-reduce | flops 16384 | bytes 98304 | tf_op jit(solution)/shard_map/psum | solution.py:63
  311.8 8.5 %all-to-all-start = ((bf16[2,16,512]{2,0,1:T(2,128)(2,1)}), bf16[2,16,512]{2,0,1:T(2,128)(2,1)S(1)}, u32[]{:S(2)}, u32[]{:S(2)}) async-start(bf16[2,16,512]{2,0,1:T(2,128)(2,1)} %bitcast.25), calls=%async_computation | async-start | bytes 65536 | tf_op jit(solution)/shard_map/all_to_all | solution.py:64
  321.0 21.9 %all-gather = bf16[16,2,512]{2,1,0:T(2,128)(2,1)S(1)} all-gather(bf16[1,2,512]{2,1,0:T(2,128)(2,1)S(1)} %slice_bitcast_fusion.12), channel_id=1, replica_groups=mesh['tm'=16,'lat'=2] {'tm'}, dimensions={0}, use_global_device_ids=true | all-gather | bytes 34816 | tf_op jit(solution)/shard_map/all_gather | solution.py:68
  344.7 11.7 %cholesky.103 = f32[128,128]{1,0:T(8,128)S(1)} custom-call(f32[128,128]{1,0:T(8,128)S(1)} %cholesky.263), custom_call_target="Cholesky" | custom-call | tf_op jit(solution)/shard_map/jit(cholesky)/cholesky | solution.py:80
  356.4 9.8 %custom-call.34 = f32[1,128,128]{1,2,0:T(8,128)S(1)} custom-call(f32[1,128,128]{2,1,0:T(8,128)S(1)} %get-tuple-element.91), custom_call_target="InvertDiagBlocksLowerTriangular" | custom-call | tf_op jit(solution)/shard_map/jit(cholesky)/cholesky | solution.py:80
  367.1 11.7 %cholesky.215 = f32[128,128]{1,0:T(8,128)S(1)} custom-call(f32[128,128]{1,0:T(8,128)S(1)} %cholesky.267), custom_call_target="Cholesky" | custom-call | tf_op jit(solution)/shard_map/jit(cholesky)/cholesky | solution.py:80
  378.8 10.2 %custom-call.35 = f32[1,128,128]{1,2,0:T(8,128)S(1)} custom-call(f32[1,128,128]{2,1,0:T(8,128)S(1)} %get-tuple-element.88), custom_call_target="InvertDiagBlocksLowerTriangular" | custom-call | tf_op jit(solution)/shard_map/jit(cholesky)/cholesky | solution.py:80
  389.7 11.7 %cholesky.236 = f32[128,128]{1,0:T(8,128)S(1)} custom-call(f32[128,128]{1,0:T(8,128)S(1)} %cholesky.272), custom_call_target="Cholesky" | custom-call | tf_op jit(solution)/shard_map/jit(cholesky)/cholesky | solution.py:80
  402.1 9.8 %custom-call.36 = f32[1,128,128]{1,2,0:T(8,128)S(1)} custom-call(f32[1,128,128]{2,1,0:T(8,128)S(1)} %get-tuple-element.85), custom_call_target="InvertDiagBlocksLowerTriangular" | custom-call | tf_op jit(solution)/shard_map/jit(cholesky)/cholesky | solution.py:80
  412.5 11.8 %cholesky.253 = f32[128,128]{1,0:T(8,128)S(1)} custom-call(f32[128,128]{1,0:T(8,128)S(1)} %convolution_subtract_fusion.5), custom_call_target="Cholesky" | custom-call | tf_op jit(solution)/shard_map/jit(cholesky)/cholesky | solution.py:80
  428.4 10.6 %while.12 = (s32[]{:T(128)}, f32[512,512]{1,0:T(8,128)S(1)}, s32[4,2]{0,1:T(2,128)S(1)}, f32[4,128,128]{2,1,0:T(8,128)}, s32[]{:T(128)}) while((s32[]{:T(128)}, f32[512,512]{1,0:T(8,128)S(1)}, s32[4,2]{0,1:T(2,128)S(1)}, f32[4,128,128]{2,1,0:T(8,128)}, s32[]{:T(128)}) %tuple.47), condition=%wide.while_cond, body=%wide.while_body.sunk | while | flops 2 | bytes 132705 | solution.py:84
  439.0 40.1 %custom-call.37 = f32[4,128,128]{1,2,0:T(8,128)S(1)} custom-call(f32[4,128,128]{2,1,0:T(8,128)} %get-tuple-element.45), custom_call_target="InvertDiagBlocksLowerTriangular" | custom-call | tf_op jit(solution)/shard_map/jit(_solve_triangular)/triangular_solve | solution.py:84
  481.3 18.2 %all-gather.1 = bf16[16,2,4096]{2,1,0:T(2,128)(2,1)S(1)} all-gather(bf16[1,2,4096]{2,1,0:T(2,128)(2,1)S(1)} %dynamic-slice_bitcast_fusion), channel_id=1, replica_groups=mesh['tm'=16,'lat'=2] {'tm'}, dimensions={0}, use_global_device_ids=true | all-gather | bytes 278528 | tf_op jit(solution)/shard_map/all_gather | solution.py:67
  509.0 13.8 %fusion.7 = f32[512,4096]{0,1:T(8,128)S(1)} fusion(f32[512,4096]{0,1:T(8,128)S(1)} %copy-done.2, f32[128,512]{1,0:T(8,128)S(1)} %fusion.58, f32[128,512]{1,0:T(8,128)S(1)} %fusion.56, f32[128,512]{1,0:T(8,128)S(1)} %fusion.54, f32[128,512]{1,0:T(8,128)S(1)} %fusion.27), kind=kOutput, calls=%fused_computation.19 | convolution fusion | flops 12887785472 | bytes 17825792 | tf_op jit(solution)/shard_map/dot_general | solution.py:92
  522.8 7.2 %select_select_fusion = f32[512,4096]{0,1:T(8,128)} fusion(f32[512,4096]{0,1:T(8,128)S(1)} %fusion.7, f32[512,512]{0,1:T(8,128)S(1)} %fusion.23, f32[512,4096]{0,1:T(8,128)S(1)} %copy-done.2, bf16[32,512]{1,0:T(8,128)(2,1)S(1)} %all_to_all.17, bf16[32,4096]{1,0:T(8,128)(2,1)S(1)} %reshape.145, f32[512]{0:T(512)S(1)} %get-tuple-element.92, ...), kind=kOutput, calls=%fused_computation.18 | convolution fusion | flops 150994944 | bytes 26534400 | tf_op jit(solution)/shard_map/dot_general | solution.py:37
  530.0 8.9 %copy.23 = f32[512,4096]{1,0:T(8,128)} copy(f32[512,4096]{0,1:T(8,128)} %select_select_fusion) | data formatting | bytes 16777216 | tf_op jit(solution)/shard_map/jit(_where)/select_n | solution.py:97
  (137 shorter events, 114.2 us)
Async XLA Ops:
  0.0 38.2 %copy-start = (bf16[2,360,1440]{2,1,0:T(8,128)(2,1)S(1)}, bf16[2,360,1440]{2,1,0:T(8,128)(2,1)}, u32[]{:S(2)}) copy-start(bf16[2,360,1440]{2,1,0:T(8,128)(2,1)} %param.7) | copy-start | bytes 6220804
  311.8 193.5 %all-to-all-start = ((bf16[2,16,512]{2,0,1:T(2,128)(2,1)}), bf16[2,16,512]{2,0,1:T(2,128)(2,1)S(1)}, u32[]{:S(2)}, u32[]{:S(2)}) async-start(bf16[2,16,512]{2,0,1:T(2,128)(2,1)} %bitcast.25), calls=%async_computation | async-start | bytes 65536 | tf_op jit(solution)/shard_map/all_to_all | solution.py:64
  505.3 3.6 copy-start.2
  522.8 16.1 %copy-start.1 = (bf16[2,360,1440]{2,1,0:T(8,128)(2,1)S(1)}, bf16[2,360,1440]{2,1,0:T(8,128)(2,1)}, u32[]{:S(2)}) copy-start(bf16[2,360,1440]{2,1,0:T(8,128)(2,1)} %param.7) | copy-start | bytes 6220804
where the time goes:
time: 548 us; the launch traced here: 539 us
  other arithmetic  308 us (56%)
  local copies, waits for them, and re-layouts  125 us (23%)
  blocking collectives  48.3 us (9%)
  matrix products  39 us (7%)
  starting transfers between devices  8.54 us (2%)
  loops' own time  5.48 us (1%)
    while x16, other arithmetic  150 us
    another operation x14, other arithmetic, on_device(): factor = jnp.linalg.cholesky(panel_gram)  79 us
    gather x8, local copies, waits for them, and re-layouts, one_part(): chosen = jnp.take(spectra, chosen_cols, axis=2)  56.9 us
    another operation x3, other arithmetic, on_device(): jax.scipy.linalg.solve_triangular(factor, row_panel.T, lower=True)  40.2 us
    dot_general x1, other arithmetic, on_device(): jnp.dot(flat, dft_basis, preferred_element_type=jnp.float32)  37.4 us
    while x8, local copies, waits for them, and re-layouts  23.9 us
    all_gather x1, blocking collectives, on_device(): lax.all_gather(coeffs[:, :PANEL], 'tm', axis=0, tiled=True)  21.9 us
    all_gather x1, blocking collectives, on_device(): lax.all_gather(local_cols, 'tm', axis=0, tiled=True)  18.2 us
  transfers between devices with their start and end apart: 1, of which 0 were waited for; matrix products, arithmetic and copies ran while one was open for 26% of the time, Pallas kernels for 0%

commit v1 on v0

v1 whole, which is shorter than its diff:
```python
import functools
import math

import jax
import jax.numpy as jnp
import ml_dtypes
import numpy as np
from jax import lax
from jax.experimental import pallas as pl
from jax.experimental.pallas import tpu as pltpu
from jax.sharding import PartitionSpec as P

LMAX = 720
PANEL = 512
CBLK = 256
KBLK = 512
LANE = 128
VMEM_LIMIT = 56 * 1024 * 1024
F32 = jnp.float32
BF16 = jnp.bfloat16


def basis_blocks(nlon):
    half = nlon // 2
    longitude = np.arange(nlon, dtype=np.int64)[:, None]
    column = np.arange(nlon, dtype=np.int64)[None, :]
    freq = column % half
    phase = (freq * longitude % nlon).astype(np.float32) * np.float32(2.0 * math.pi / nlon)
    table = np.where(column < half, np.cos(phase), np.sin(phase)).astype(ml_dtypes.bfloat16)
    blocks = -(-nlon // CBLK)
    padded = np.zeros((nlon, blocks * CBLK), ml_dtypes.bfloat16)
    padded[:, :nlon] = table
    return np.ascontiguousarray(padded.reshape(nlon, blocks, CBLK).transpose(1, 0, 2))


def one_hot(column, start, rows):
    ids = lax.broadcasted_iota(jnp.int32, (rows, column.shape[1]), 0)
    return jnp.where(ids == column - start, 1.0, 0.0).astype(BF16)


def latitude_sums(chosen, weights, times):
    lats = weights.shape[0]
    sums = [
        jnp.sum(chosen[t * lats : (t + 1) * lats] * weights, axis=0, keepdims=True)
        for t in range(times)
    ]
    return jnp.concatenate(sums, axis=0)


def spectra_kernel(scale, fields_ref, basis_ref, column_ref, weights_ref, spectra_ref, part_ref, chosen_ref):
    step = pl.program_id(0)
    times = fields_ref.shape[0]
    block = jnp.concatenate(
        [jnp.dot(fields_ref[t], basis_ref[0], preferred_element_type=F32) for t in range(times)], axis=0
    )
    block = (block * scale).astype(BF16)
    spectra_ref[...] = block
    hot = one_hot(column_ref[...], step * CBLK, CBLK)
    term = jnp.dot(block, hot, preferred_element_type=F32)

    @pl.when(step == 0)
    def _():
        chosen_ref[...] = term

    @pl.when(step > 0)
    def _():
        chosen_ref[...] += term

    @pl.when(step == pl.num_programs(0) - 1)
    def _():
        part_ref[...] = latitude_sums(chosen_ref[...], weights_ref[...].astype(F32), times)


def spectra_and_panel(fields, basis, column, legendre):
    times, lats, nlon = fields.shape
    blocks = basis.shape[0]
    rows = times * lats
    return pl.pallas_call(
        functools.partial(spectra_kernel, 1.0 / math.sqrt(nlon)),
        grid=(blocks,),
        in_specs=[
            pl.BlockSpec((times, lats, nlon), lambda i: (0, 0, 0)),
            pl.BlockSpec((1, nlon, CBLK), lambda i: (i, 0, 0)),
            pl.BlockSpec((1, PANEL), lambda i: (0, 0)),
            pl.BlockSpec((lats, PANEL), lambda i: (0, 0)),
        ],
        out_specs=[
            pl.BlockSpec((rows, CBLK), lambda i: (0, i)),
            pl.BlockSpec((times, PANEL), lambda i: (0, 0)),
        ],
        out_shape=[
            jax.ShapeDtypeStruct((rows, blocks * CBLK), BF16),
            jax.ShapeDtypeStruct((times, PANEL), F32),
        ],
        scratch_shapes=[pltpu.VMEM((rows, PANEL), F32)],
        compiler_params=pltpu.CompilerParams(vmem_limit_bytes=VMEM_LIMIT),
        cost_estimate=pl.CostEstimate(
            flops=2 * rows * blocks * CBLK * (nlon + PANEL), bytes_accessed=8 << 20, transcendentals=0
        ),
        name="spectra_and_panel",
    )(fields, basis, column, legendre)


def contract_kernel(times, spectra_ref, column_ref, weights_ref, part_ref):
    hot = one_hot(column_ref[...], 0, spectra_ref.shape[1])
    chosen = jnp.dot(spectra_ref[...], hot, preferred_element_type=F32)
    part_ref[...] = latitude_sums(chosen, weights_ref[...].astype(F32), times)


def contract_rest(spectra, column, legendre, times):
    rows, cols = spectra.shape
    lats, kcoef = legendre.shape
    first = PANEL // KBLK
    steps = kcoef // KBLK - first
    return pl.pallas_call(
        functools.partial(contract_kernel, times),
        grid=(steps,),
        in_specs=[
            pl.BlockSpec((rows, cols), lambda i: (0, 0)),
            pl.BlockSpec((1, KBLK), lambda i: (0, i + first)),
            pl.BlockSpec((lats, KBLK), lambda i: (0, i + first)),
        ],
        out_specs=pl.BlockSpec((times, KBLK), lambda i: (0, i)),
        out_shape=jax.ShapeDtypeStruct((times, steps * KBLK), F32),
        compiler_params=pltpu.CompilerParams(vmem_limit_bytes=VMEM_LIMIT),
        cost_estimate=pl.CostEstimate(
            flops=2 * rows * cols * steps * KBLK, bytes_accessed=8 << 20, transcendentals=0
        ),
        name="contract_rest",
    )(spectra, column, legendre)


def split(value, pieces):
    out = []
    for _ in range(pieces):
        piece = value.astype(BF16)
        out.append(piece)
        value = value - piece.astype(F32)
    return out


def panel_kernel(coef_ref, lam_ref, w_ref, diag_ref, inverse_ref, q_ref, g_ref, y_ref, x_ref, z_ref):
    nt = coef_ref.shape[0]
    lanes = PANEL + LANE
    coef = coef_ref[...]
    lam = lam_ref[...]
    scaled = coef / lam
    starts, total = [], 0
    for r in range(nt):
        low = r // 8 * 8
        z_ref[total : total + nt - low, :] = coef[low:, :] * scaled[r : r + 1, :]
        starts.append(total)
        total += nt - low
    ids = lax.broadcasted_iota(jnp.int32, (PANEL, lanes), 0)
    upto = lax.broadcasted_iota(jnp.int32, (PANEL, lanes), 1)
    tri = jnp.where(ids < upto, 1.0, 0.0).astype(BF16)
    prefix = 0.0
    for piece in split(z_ref[...], 3)[::-1]:
        prefix = prefix + jnp.dot(piece, tri, preferred_element_type=F32)
    q_ref[...] = prefix
    y_ref[:, :PANEL] = coef
    eye = lax.broadcasted_iota(jnp.int32, (nt, LANE), 0) == lax.broadcasted_iota(jnp.int32, (nt, LANE), 1)
    y_ref[:, PANEL:] = jnp.where(eye, 1.0, 0.0)
    inverses = []
    for r in range(nt):
        low = r // 8 * 8
        place = low + lax.broadcasted_iota(jnp.int32, (nt - low, lanes), 0)
        row = q_ref[starts[r] : starts[r] + nt - low, :] + jnp.where(place == r, float(nt), 0.0)
        for p in range(r):
            base = starts[p] + low - p // 8 * 8
            factor = g_ref[starts[p] + r - p // 8 * 8 : starts[p] + r - p // 8 * 8 + 1, :]
            row = row - factor * q_ref[base : base + nt - low, :]
        q_ref[starts[r] : starts[r] + nt - low, :] = row
        inv = 1.0 / row[r - low : r - low + 1, :]
        inverses.append(inv)
        ratio = jnp.where(place > r, row * inv, 0.0)
        g_ref[starts[r] : starts[r] + nt - low, :] = ratio
        y_ref[low:, :] = y_ref[low:, :] - ratio * y_ref[r : r + 1, :]
    x_ref[...] = jnp.zeros_like(x_ref)
    for r in range(nt - 1, -1, -1):
        low = r // 8 * 8
        ratio = g_ref[starts[r] : starts[r] + nt - low, :]
        tail = jnp.sum(ratio * x_ref[low:, :], axis=0, keepdims=True)
        x_ref[r : r + 1, :] = y_ref[r : r + 1, :] * inverses[r] - tail
    solved = x_ref[:, :PANEL]
    pivot = jnp.sqrt(lam + jnp.sum(coef * solved, axis=0, keepdims=True))
    w_ref[...] = solved / pivot
    diag_ref[...] = lam / pivot
    inverse_ref[...] = x_ref[:, PANEL:]


def panel_small(coef, lam):
    nt = coef.shape[0]
    rows = sum(nt - r // 8 * 8 for r in range(nt))
    lanes = PANEL + LANE
    return pl.pallas_call(
        panel_kernel,
        out_shape=[
            jax.ShapeDtypeStruct((nt, PANEL), F32),
            jax.ShapeDtypeStruct((1, PANEL), F32),
            jax.ShapeDtypeStruct((nt, LANE), F32),
        ],
        scratch_shapes=[
            pltpu.VMEM((rows, lanes), F32),
            pltpu.VMEM((rows, lanes), F32),
            pltpu.VMEM((nt, lanes), F32),
            pltpu.VMEM((nt, lanes), F32),
            pltpu.VMEM((rows, PANEL), F32),
        ],
        compiler_params=pltpu.CompilerParams(vmem_limit_bytes=VMEM_LIMIT),
        cost_estimate=pl.CostEstimate(flops=4 << 30, bytes_accessed=1 << 18, transcendentals=0),
        name="panel_small",
    )(coef, lam)


def panel_large(coef, lam):
    nt = coef.shape[0]
    gram = jnp.dot(coef.T, coef, precision=lax.Precision.HIGHEST) / nt + jnp.diag(lam[0])
    factor = jnp.linalg.cholesky(gram)
    solved = jax.scipy.linalg.solve_triangular(factor, coef.T, lower=True)
    w = solved.T / nt
    rest = jnp.eye(nt, dtype=F32) / nt - jnp.dot(w, w.T, precision=lax.Precision.HIGHEST)
    pivot = jnp.diagonal(factor)[None, :]
    pad = -(-nt // LANE) * LANE - nt
    return w, pivot - jnp.sum(coef * w, axis=0, keepdims=True), jnp.pad(rest, ((0, 0), (0, pad)))


def stack_pieces(value):
    high, low = split(value, 2)
    return jnp.concatenate([high.astype(F32), low.astype(F32)], axis=0).astype(BF16)


def twice(value):
    return jnp.concatenate([value, value], axis=0).astype(BF16)


def contract_times(left, right):
    return lax.dot_general(left, right, (((0,), (0,)), ((), ())), preferred_element_type=F32)


def tile_kernel(place_ref, rows_ref, cols_ref, w_ref, wrows_ref, diag_ref, lam_ref, inverse_ref, out_ref):
    height, width = out_ref.shape
    nt = rows_ref.shape[0]
    row_start = place_ref[0]
    col_start = place_ref[1] + pl.program_id(0) * width
    row_ids = row_start + lax.broadcasted_iota(jnp.int32, (height, width), 0)
    col_ids = col_start + lax.broadcasted_iota(jnp.int32, (height, width), 1)
    in_panel_rows = row_start < PANEL
    in_panel_cols = col_start < PANEL

    @pl.when(in_panel_cols)
    def _():
        value = contract_times(twice(rows_ref[...]), stack_pieces(w_ref[...]))
        value = jnp.where(row_ids >= col_ids, value, 0.0)
        out_ref[...] = value + jnp.where(row_ids == col_ids, diag_ref[...], 0.0)

    @pl.when(jnp.logical_not(in_panel_cols) & in_panel_rows)
    def _():
        out_ref[...] = contract_times(stack_pieces(wrows_ref[...]), twice(cols_ref[...]))

    @pl.when(jnp.logical_not(in_panel_cols) & jnp.logical_not(in_panel_rows))
    def _():
        cols = cols_ref[...]
        turned = contract_times(stack_pieces(inverse_ref[:, :nt]), twice(cols))
        value = contract_times(twice(rows_ref[...]), stack_pieces(turned))
        out_ref[...] = value + jnp.where(row_ids == col_ids, lam_ref[...], 0.0)


def out_tile(place, rows, cols, w, wrows, diag, lam_cols, inverse):
    nt, height = rows.shape
    width = cols.shape[1]
    block = min(PANEL, width)
    whole = lambda i: (0, 0)
    part = lambda i: (0, i)
    return pl.pallas_call(
        tile_kernel,
        grid=(width // block,),
        in_specs=[
            pl.BlockSpec(memory_space=pltpu.SMEM),
            pl.BlockSpec((nt, height), whole),
            pl.BlockSpec((nt, block), part),
            pl.BlockSpec((nt, PANEL), whole),
            pl.BlockSpec((nt, height), whole),
            pl.BlockSpec((1, PANEL), whole),
            pl.BlockSpec((1, block), part),
            pl.BlockSpec(inverse.shape, whole),
        ],
        out_specs=pl.BlockSpec((height, block), part),
        out_shape=jax.ShapeDtypeStruct((height, width), F32),
        compiler_params=pltpu.CompilerParams(vmem_limit_bytes=VMEM_LIMIT),
        cost_estimate=pl.CostEstimate(
            flops=4 * nt * height * width, bytes_accessed=4 * height * width, transcendentals=0
        ),
        name="out_tile",
    )(place, rows, cols, w, wrows, diag, lam_cols, inverse)


def on_device(basis, fields, legendre, order_table, window_start, ridge):
    times, lats, nlon = fields.shape
    kcoef = legendre.shape[1]
    tm_count, lat_count = lax.axis_size("tm"), lax.axis_size("lat")
    nt = times * tm_count
    rows_width, cols_width = kcoef // tm_count, kcoef // lat_count
    tm_index, lat_index = lax.axis_index("tm"), lax.axis_index("lat")
    window = lax.dynamic_slice_in_dim(order_table, window_start[0], kcoef, 1)
    degree = window[0:1]
    column = window[1:2] + nlon // 2 * window[2:3]
    lam = ridge[0] * (1.0 + (degree * (degree + 1)).astype(F32) / float(LMAX * (LMAX + 1)))
    spare = -lats % 8
    if spare:
        fields = jnp.pad(fields, ((0, 0), (0, spare), (0, 0)))
        legendre = jnp.pad(legendre, ((0, spare), (0, 0)))

    spectra, panel_part = spectra_and_panel(fields, basis, column, legendre)
    everyone = ("tm", "lat")
    sent = jnp.broadcast_to(panel_part[None], (tm_count * lat_count, times, PANEL))
    arrived = lax.all_to_all(sent, everyone, 0, 0).reshape(tm_count, lat_count, times, PANEL)
    panel_coef = jnp.sum(arrived, axis=1).astype(BF16).astype(F32).reshape(nt, PANEL)

    rest_part = contract_rest(spectra, column, legendre, times)
    part = jnp.concatenate([panel_part, rest_part], axis=1)
    coef = lax.psum(part, "lat").astype(BF16)
    cols_own = lax.dynamic_slice_in_dim(coef, lat_index * cols_width, cols_width, 1)
    wanted = jnp.concatenate(
        [
            jnp.broadcast_to(cols_own[None], (tm_count, times, cols_width)),
            coef.reshape(times, tm_count, rows_width).transpose(1, 0, 2),
        ],
        axis=2,
    )
    got = lax.all_to_all(wanted, "tm", 0, 0).reshape(nt, cols_width + rows_width)
    cols, rows = got[:, :cols_width].astype(F32), got[:, cols_width:].astype(F32)

    lam_panel = lam[:, :PANEL]
    w, diag, inverse = (panel_small if nt <= 32 else panel_large)(panel_coef, lam_panel)
    row_start, col_start = tm_index * rows_width, lat_index * cols_width
    wrows = lax.dynamic_slice_in_dim(w, jnp.minimum(row_start, PANEL - rows_width), rows_width, 1)
    lam_cols = lax.dynamic_slice_in_dim(lam, col_start, cols_width, 1)
    place = jnp.stack([row_start, col_start]).astype(jnp.int32)
    return out_tile(place, rows, cols, w, wrows, diag, lam_cols, inverse)


def solution(mesh):
    def run(fields, legendre, order_table, window_start, ridge):
        basis = jnp.asarray(basis_blocks(fields.shape[2]))
        placed = (P(), P("tm", "lat", None), P("lat", None), P(), P(), P())
        body = jax.shard_map(on_device, mesh=mesh, in_specs=placed, out_specs=P("tm", "lat"), check_vma=False)
        return body(basis, fields, legendre, order_table, window_start, ridge)

    return run
```

time: 548 us -> 84.3 us (0.15); the launches traced: 539 us -> 83.1 us
  other arithmetic: 308 us -> 6.78 us
  local copies, waits for them, and re-layouts: 125 us -> 3.57 us
  Pallas kernels: 0 us -> 46.2 us
  blocking collectives: 48.3 us -> 7.03 us
  matrix products: 39 us -> 0 us
  starting transfers between devices: 8.54 us -> 15 us
  loops' own time: 5.48 us -> 0 us
    while x16 -> x0, other arithmetic: 150 us -> none
    another operation x17 -> x1, other arithmetic: 119 us -> 0.59 us  [on_device(): place = jnp.stack([row_start, col_start]).astype(jnp.int32)]
    gather x8 -> x0, local copies, waits for them, and re-layouts: 56.9 us -> none  [one_part(): chosen = jnp.take(spectra, chosen_cols, axis=2)]
    pallas_call x0 -> x4, Pallas kernels: none -> 46.2 us  [the longest x1 22.6 us: contract_rest(): pl.pallas_call(functools.partial(contract_kernel, times), grid=(steps,),...]
    all_gather x2 -> x0, blocking collectives: 40.1 us -> none  [the longest x1 21.9 us: on_device(): lax.all_gather(coeffs[:, :PANEL], 'tm', axis=0, tiled=True)]
    dot_general x1 -> x0, other arithmetic: 37.4 us -> none  [on_device(): jnp.dot(flat, dft_basis, preferred_element_type=jnp.float32)]
    dot_general x6 -> x0, matrix products: 32.5 us -> none  [the longest x1 13.8 us: on_device(): update = jnp.dot(panel_rows, upper, precision=lax.Precision.HIGHEST)]
    while x9 -> x0, local copies, waits for them, and re-layouts: 31.8 us -> none
  transfers between devices with their start and end apart: 1 -> 2, of which waited for: 0 -> 1; matrix products, arithmetic and copies ran while one was open for 26% -> 7% of each run, Pallas kernels for 0% -> 35%
where the time goes in v1:
time: 84.3 us; the launch traced here: 83.1 us
  Pallas kernels  46.2 us (55%)
  starting transfers between devices  15 us (18%)
  blocking collectives  7.03 us (8%)
  other arithmetic  6.78 us (8%)
  local copies, waits for them, and re-layouts  3.57 us (4%)
  waiting for transfers between devices  3.19 us (4%)
  between operations  1.39 us (2%)
    pallas_call x1, Pallas kernels, contract_rest(): pl.pallas_call(functools.partial(contract_kernel, times), grid=(steps,),...  22.6 us
    pallas_call x1, Pallas kernels, spectra_and_panel(): pl.pallas_call(functools.partial(spectra_kernel, 1.0 / math.sqrt(nlon)),...  9.87 us
    all_to_all x1, starting transfers between devices, on_device(): lax.all_to_all(wanted, 'tm', 0, 0).reshape(nt, cols_width + rows_width)  7.93 us
    pallas_call x1, Pallas kernels, out_tile(): pl.pallas_call(tile_kernel, grid=(width // block,), in_specs=[pl.BlockSpe...  7.6 us
    all_to_all x1, starting transfers between devices, on_device(): lax.all_to_all(sent, everyone, 0, 0)  7.09 us
    psum x1, blocking collectives, on_device(): coef = lax.psum(part, 'lat').astype(BF16)  7.03 us
    pallas_call x1, Pallas kernels, panel_small(): pl.pallas_call(panel_kernel, out_shape=[jax.ShapeDtypeStruct((nt, PANEL),...  6.06 us
    all_to_all x1, waiting for transfers between devices, on_device(): lax.all_to_all(wanted, 'tm', 0, 0).reshape(nt, cols_width + rows_width)  3.19 us
  transfers between devices with their start and end apart: 2, of which 1 were waited for; matrix products, arithmetic and copies ran while one was open for 7% of the time, Pallas kernels for 35%

profile of v1, /device:TPU:1, one launch (start us, length us, event | category | flops | bytes accessed | tf_op | source)
XLA Modules:
  0.0 83.1 jit_solution(9465256668963737312)
XLA Ops:
  0.7 1.8 %fusion.5.column_ref = s32[1,8192]{1,0:T(1,128)} fusion(s32[3,16384]{1,0:T(4,128)} %param.8, s32[]{:T(128)S(6)} %add.34, s32[]{:T(128)S(6)} %select_n.8, s32[]{:T(128)S(6)} %add.33), kind=kLoop, calls=%fused_computation.13 | loop fusion | flops 16384 | bytes 98316 | tf_op jit(solution)/shard_map/add | solution.py:307
  2.5 9.9 %spectra_and_panel.1 = (bf16[720,1536]{1,0:T(8,128)(2,1)}, f32[2,512]{1,0:T(2,128)}) custom-call(bf16[2,360,1440]{2,1,0:T(8,128)(2,1)} %fields_ref.1, bf16[6,1440,256]{2,1,0:T(8,128)(2,1)} %constant.31.clone.basis_ref, s32[1,8192]{1,0:T(1,128)} %fusion.5.column_ref, bf16[360,8192]{1,0:T(8,128)(2,1)} %weights_ref.3), custom_call_target="tpu_custom_call" | custom-call | flops 4317511680 | bytes 8388608 | tf_op jit(solution)/shard_map/spectra_and_panel/pallas_call | solution.py:78
  12.3 1.3 %broadcast_in_dim.5 = f32[32,2,512]{2,1,0:T(2,128)} broadcast(f32[2,512]{1,0:T(2,128)} %get-tuple-element.10), dimensions={1,2} | broadcast | bytes 135168 | tf_op jit(solution)/shard_map/broadcast_in_dim | solution.py:316
  13.7 7.1 %all-to-all-start.1 = ((f32[32,2,512]{2,1,0:T(2,128)}), f32[32,2,512]{2,1,0:T(2,128)S(1)}, u32[]{:S(2)}, u32[]{:S(2)}) async-start(f32[32,2,512]{2,1,0:T(2,128)} %broadcast_in_dim.5), calls=%async_computation.1 | async-start | bytes 262144 | tf_op jit(solution)/shard_map/all_to_all | solution.py:317
  21.4 1.1 %fusion.3 = f32[1,8192]{1,0:T(1,128)S(1)} fusion(s32[3,16384]{1,0:T(4,128)} %param.8, s32[]{:T(128)S(6)} %select_n.8, f32[]{:T(128)} %bitcast.12), kind=kLoop, calls=%fused_computation.9 | loop fusion | flops 49152 | bytes 65544 | tf_op jit(solution)/shard_map/mul | solution.py:308
  22.5 0.0 copy-start
  22.5 22.6 %contract_rest.1 = f32[2,7680]{1,0:T(2,128)} custom-call(bf16[720,1536]{1,0:T(8,128)(2,1)} %get-tuple-element.11.spectra_ref, s32[1,8192]{1,0:T(1,128)} %fusion.5.column_ref, bf16[360,8192]{1,0:T(8,128)(2,1)} %weights_ref.3), custom_call_target="tpu_custom_call" | custom-call | flops 16986931200 | bytes 8388608 | tf_op jit(solution)/shard_map/contract_rest/pallas_call | solution.py:115
  45.1 0.0 copy-done
  45.1 0.9 %pad_maximum_fusion.1 = f32[2,8192]{1,0:T(2,128)S(1)} fusion(f32[2,7680]{1,0:T(2,128)} %contract_rest.1, f32[2,512]{1,0:T(2,128)S(1)} %copy-done), kind=kLoop, calls=%fused_computation.3 | loop fusion | flops 16384 | bytes 131072 | tf_op jit(solution)/shard_map/concatenate | solution.py:321
  46.0 7.0 %psum.7 = bf16[2,8192]{1,0:T(2,128)(2,1)S(1)} all-reduce(f32[2,8192]{1,0:T(2,128)S(1)} %pad_maximum_fusion.1), channel_id=1, replica_groups=mesh['tm'=16,'lat'=2] {'lat'}, use_global_device_ids=true, to_apply=%region_0.0 | all-reduce | flops 16384 | bytes 98304 | tf_op jit(solution)/shard_map/psum | solution.py:322
  53.1 0.2 broadcast_in_dim.4
  53.3 1.0 %pad_maximum_fusion = bf16[16,2,4608]{2,1,0:T(2,128)(2,1)} fusion(bf16[16,2,512]{2,1,0:T(2,128)(2,1)S(1)} %bitcast.13, bf16[16,2,4096]{2,1,0:T(2,128)(2,1)S(1)} %broadcast_in_dim.4), kind=kLoop, calls=%fused_computation | loop fusion | flops 589824 | bytes 589824 | tf_op jit(solution)/shard_map/concatenate | solution.py:324
  54.2 0.6 constant_dynamic-slice_fusion.lam_ref
  54.8 0.6 slice.26.lam_ref
  55.4 0.6 pad_add_fusion.place_ref
  56.0 0.0 all-to-all-done.1
  56.0 7.9 %all-to-all-start = ((bf16[16,2,4608]{2,1,0:T(2,128)(2,1)}), bf16[16,2,4608]{2,1,0:T(2,128)(2,1)S(1)}, u32[]{:S(2)}, u32[]{:S(2)}) async-start(bf16[16,2,4608]{2,1,0:T(2,128)(2,1)} %pad_maximum_fusion), calls=%async_computation | async-start | bytes 589824 | tf_op jit(solution)/shard_map/all_to_all | solution.py:331
  63.9 0.1 bitcast_reduce_fusion
  64.0 0.1 copy.12
  64.1 0.7 reshape.19.coef_ref
  64.7 6.1 %panel_small.1 = (f32[32,512]{1,0:T(8,128)}, f32[1,512]{1,0:T(1,128)}, f32[32,128]{1,0:T(8,128)}) custom-call(f32[32,512]{1,0:T(8,128)} %reshape.19.coef_ref, f32[1,512]{1,0:T(1,128)} %slice.26.lam_ref), custom_call_target="tpu_custom_call" | custom-call | flops 4294967296 | bytes 262144 | tf_op jit(solution)/shard_map/panel_small/pallas_call | solution.py:196
  70.8 3.2 %all-to-all-done = bf16[16,2,4608]{2,1,0:T(2,128)(2,1)S(1)} async-done(((bf16[16,2,4608]{2,1,0:T(2,128)(2,1)}), bf16[16,2,4608]{2,1,0:T(2,128)(2,1)S(1)}, u32[]{:S(2)}, u32[]{:S(2)}) %all-to-all-start) | async-done | bytes 294944 | tf_op jit(solution)/shard_map/all_to_all | solution.py:331
  74.0 0.1 reshape.17
  74.1 0.6 slice_convert_fusion.1.rows_ref
  74.7 0.8 slice_convert_fusion.cols_ref
  75.5 7.6 %out_tile.1 = f32[512,4096]{1,0:T(8,128)} custom-call(s32[2]{0:T(128)} %pad_add_fusion.place_ref, f32[32,512]{1,0:T(8,128)} %slice_convert_fusion.1.rows_ref, f32[32,4096]{1,0:T(8,128)} %slice_convert_fusion.cols_ref, f32[32,512]{1,0:T(8,128)} %get-tuple-element.12.w_ref.wrows_ref, f32[32,512]{1,0:T(8,128)} %get-tuple-element.12.w_ref.wrows_ref, ...), custom_call_target="tpu_custom_call" | custom-call | flops 268435456 | bytes 8388608 | tf_op jit(solution)/shard_map/out_tile/pallas_call | solution.py:275
  (2 shorter events, 0.0 us)
Async XLA Ops:
  13.7 42.3 %all-to-all-start.1 = ((f32[32,2,512]{2,1,0:T(2,128)}), f32[32,2,512]{2,1,0:T(2,128)S(1)}, u32[]{:S(2)}, u32[]{:S(2)}) async-start(f32[32,2,512]{2,1,0:T(2,128)} %broadcast_in_dim.5), calls=%async_computation.1 | async-start | bytes 262144 | tf_op jit(solution)/shard_map/all_to_all | solution.py:317
  22.5 22.6 %copy-start = (f32[2,512]{1,0:T(2,128)S(1)}, f32[2,512]{1,0:T(2,128)}, u32[]{:S(2)}) copy-start(f32[2,512]{1,0:T(2,128)} %get-tuple-element.10) | copy-start | bytes 12292
  56.0 18.0 %all-to-all-start = ((bf16[16,2,4608]{2,1,0:T(2,128)(2,1)}), bf16[16,2,4608]{2,1,0:T(2,128)(2,1)S(1)}, u32[]{:S(2)}, u32[]{:S(2)}) async-start(bf16[16,2,4608]{2,1,0:T(2,128)(2,1)} %pad_maximum_fusion), calls=%async_computation | async-start | bytes 589824 | tf_op jit(solution)/shard_map/all_to_all | solution.py:331

commit v2 on v1

v2 whole, which is shorter than its diff:
```python
import functools
import math

import jax
import jax.numpy as jnp
import ml_dtypes
import numpy as np
from jax import lax
from jax.experimental import pallas as pl
from jax.experimental.pallas import tpu as pltpu
from jax.sharding import PartitionSpec as P

LMAX = 720
PANEL = 512
LANE = 128
SUB = 8
GATHER = 256
STEP = 1024
TRANSFORMS = 3
VMEM_LIMIT = 56 * 1024 * 1024
F32 = jnp.float32
BF16 = jnp.bfloat16


def basis_table(nlon):
    half = nlon // 2
    column = np.arange(nlon, dtype=np.int64)[:, None]
    longitude = np.arange(nlon, dtype=np.int64)[None, :]
    phase = (column % half * longitude % nlon).astype(np.float32) * np.float32(2.0 * math.pi / nlon)
    return np.where(column < half, np.cos(phase), np.sin(phase)).astype(ml_dtypes.bfloat16)


def pick_rows(column_ref, start, table_ref, picked_ref):
    for j in range(GATHER):
        group = pl.multiple_of(column_ref[start + j], SUB)
        picked_ref[SUB * j : SUB * (j + 1), :] = table_ref[pl.ds(group, SUB), :]


def latitude_sums(picked_ref, weights, times):
    lats = weights.shape[0]
    pieces = -(-lats // LANE)
    sums = []
    for t in range(times):
        rows = [picked_ref[pl.ds(pieces * t + s, GATHER, stride=SUB), :] for s in range(pieces)]
        value = jnp.concatenate(rows, axis=1).astype(BF16)[:, :lats]
        every = jnp.dot(value, weights, preferred_element_type=F32)
        own = []
        for low in range(0, GATHER, LANE):
            square = every[low : low + LANE, low : low + LANE]
            shape = (LANE, LANE)
            eye = lax.broadcasted_iota(jnp.int32, shape, 0) == lax.broadcasted_iota(jnp.int32, shape, 1)
            own.append(jnp.sum(jnp.where(eye, square, 0.0), axis=0, keepdims=True))
        sums.append(jnp.concatenate(own, axis=1))
    return jnp.concatenate(sums, axis=0)


def contract_block(place, width, step, first, last, column_ref, table_ref, weights_ref, sums_ref, even_ref, odd_ref):
    times = sums_ref.shape[0]
    picked = [even_ref, odd_ref]

    @pl.when(step == first)
    def _():
        pick_rows(column_ref, place(0), table_ref, even_ref)

    for part in range(width // GATHER):
        low = part * GATHER
        if low + GATHER < width:
            after = place(step - first) + low + GATHER
        else:
            after = place(jnp.minimum(step + 1, last) - first)
        pick_rows(column_ref, after, table_ref, picked[(part + 1) % 2])
        at = pl.multiple_of((step - first) * width + low, GATHER)
        sums_ref[:, pl.ds(at, GATHER)] = latitude_sums(
            picked[part % 2], weights_ref[:, low : low + GATHER], times
        )


class Plan:
    def __init__(self, kcoef, tm_count, lat_count, times, skip, take, with_panel):
        self.tm_count, self.lat_count, self.times = tm_count, lat_count, times
        self.skip, self.take = skip, take
        self.part_width, self.rows_width = kcoef // lat_count, kcoef // tm_count
        self.width = min(STEP, take)
        self.per_part = take // self.width
        self.steps = self.per_part * lat_count
        self.col_tiles, self.row_tiles = take // LANE, self.rows_width // LANE
        self.panel_tiles = PANEL // LANE if with_panel else 0
        self.first_panel = self.col_tiles + self.row_tiles
        self.across = -(-(self.first_panel + self.panel_tiles) // SUB)
        self.slab = (times * SUB, self.across * LANE)
        self.shape = (tm_count * lat_count,) + self.slab
        self.sums_shape = (self.across, tm_count * self.slab[0], LANE)

    def place(self, i):
        return i // self.per_part * self.part_width + self.skip + i % self.per_part * self.width

    def block(self, i):
        return i // self.per_part * (self.part_width // self.width) + self.skip // self.width + i % self.per_part

    def rows_place(self, owner):
        part, low = divmod(owner * self.rows_width, self.part_width)
        low -= self.skip
        return part * self.take + low if 0 <= low < self.take else None

    def holds_rows(self, tm_index):
        low = tm_index * self.rows_width % self.part_width - self.skip
        return (low >= 0) & (low < self.take)

    def spot(self, tile, time):
        low = tile % self.across * LANE
        return time * SUB + tile // self.across, slice(low, low + LANE)

    def pack(self, sums_ref, slab_ref, sent_ref):
        def fill(tile, source, count):
            for n in range(count):
                for t in range(self.times):
                    row, lanes = self.spot(tile + n, t)
                    low = source + n * LANE
                    slab_ref[row : row + 1, lanes] = sums_ref[t : t + 1, low : low + LANE]

        slab_ref[...] = jnp.zeros_like(slab_ref)
        fill(self.first_panel, 0, self.panel_tiles)
        for part in range(self.lat_count):
            fill(0, part * self.take, self.col_tiles)
            for owner in range(self.tm_count):
                source = self.rows_place(owner)
                if source is not None:
                    fill(self.col_tiles, source, self.row_tiles)
                sent_ref[owner * self.lat_count + part] = slab_ref[...].astype(BF16)

    def gather_sums(self, got_ref, slabs_ref):
        rows = self.slab[0]
        for sender in range(self.tm_count):
            first = sender * self.lat_count
            total = got_ref[first].astype(F32)
            for part in range(1, self.lat_count):
                total = total + got_ref[first + part].astype(F32)
            for n in range(self.across):
                slabs_ref[n, sender * rows : (sender + 1) * rows, :] = total[:, n * LANE : (n + 1) * LANE]

    def tile(self, slabs_ref, tile):
        pieces = []
        for t in range(self.times):
            row = t * SUB + tile // self.across
            pieces.append(slabs_ref[tile % self.across, pl.ds(row, self.tm_count, stride=self.slab[0]), :])
        return jnp.concatenate(pieces, axis=0).astype(BF16).astype(F32)

    def unpack(self, got):
        split_shape = (self.tm_count, self.lat_count, self.times, SUB * self.across * LANE)
        total = got.astype(F32).reshape(split_shape).sum(axis=1).astype(BF16).astype(F32)
        return total.transpose(1, 0, 2).reshape(self.times * self.tm_count, -1)


def spectra_kernel(plan, scale, transforms, column_ref, fields_ref, basis_ref, weights_ref, sent_ref, kept_ref,
                   lines_ref, table_ref, even_ref, odd_ref, sums_ref, slab_ref, kept_sem):
    step = pl.program_id(0)
    last = pl.num_programs(0) - 1
    times, lats, _ = fields_ref.shape
    pieces = -(-lats // LANE)
    rows = basis_ref.shape[0]
    keep = pltpu.make_async_copy(table_ref, kept_ref, kept_sem)

    @pl.when(step == 0)
    def _():
        for t in range(times):
            lines_ref[pieces * LANE * t : pieces * LANE * t + lats, :] = fields_ref[t]

    @pl.when(step < transforms)
    def _():
        spectra = scale * lax.dot_general(
            basis_ref[...], lines_ref[...], (((1,), (1,)), ((), ())), preferred_element_type=F32
        )
        for s in range(times * pieces):
            table_ref[pl.ds(step * rows * SUB + s, rows, stride=SUB), :] = spectra[:, LANE * s : LANE * (s + 1)]

    @pl.when(step == transforms - 1)
    def _():
        keep.start()

    @pl.when(step >= transforms)
    def _():
        contract_block(plan.place, plan.width, step, transforms, last, column_ref, table_ref, weights_ref,
                       sums_ref, even_ref, odd_ref)

    @pl.when(step == last)
    def _():
        plan.pack(sums_ref, slab_ref, sent_ref)
        keep.wait()


def contract_kernel(plan, column_ref, table_ref, weights_ref, sent_ref, even_ref, odd_ref, sums_ref, slab_ref):
    step = pl.program_id(0)
    last = pl.num_programs(0) - 1
    contract_block(plan.place, plan.width, step, 0, last, column_ref, table_ref, weights_ref, sums_ref,
                   even_ref, odd_ref)

    @pl.when(step == last)
    def _():
        plan.pack(sums_ref, slab_ref, sent_ref)


def contract_scratch(plan):
    return [
        pltpu.VMEM((GATHER * SUB, LANE), F32),
        pltpu.VMEM((GATHER * SUB, LANE), F32),
        pltpu.VMEM((plan.times, plan.steps * plan.width), F32),
        pltpu.VMEM(plan.slab, F32),
    ]


def spectra_and_contract(plan, fields, basis, column, legendre):
    times, lats, nlon = fields.shape
    pieces = -(-lats // LANE)
    rows = nlon // TRANSFORMS
    later = lambda i: jnp.maximum(i - TRANSFORMS, 0)
    return pl.pallas_call(
        functools.partial(spectra_kernel, plan, 1.0 / math.sqrt(nlon), TRANSFORMS),
        grid_spec=pltpu.PrefetchScalarGridSpec(
            num_scalar_prefetch=1,
            grid=(TRANSFORMS + plan.steps,),
            in_specs=[
                pl.BlockSpec((times, lats, nlon), lambda i, c: (0, 0, 0)),
                pl.BlockSpec((rows, nlon), lambda i, c: (jnp.minimum(i, TRANSFORMS - 1), 0)),
                pl.BlockSpec((lats, plan.width), lambda i, c: (0, plan.block(later(i)))),
            ],
            out_specs=[
                pl.BlockSpec(plan.shape, lambda i, c: (0, 0, 0)),
                pl.BlockSpec(memory_space=pl.ANY),
            ],
            scratch_shapes=[
                pltpu.VMEM((times * pieces * LANE, nlon), BF16),
                pltpu.VMEM((nlon * SUB, LANE), F32),
                *contract_scratch(plan),
                pltpu.SemaphoreType.DMA(()),
            ],
        ),
        out_shape=[
            jax.ShapeDtypeStruct(plan.shape, BF16),
            jax.ShapeDtypeStruct((nlon * SUB, LANE), F32),
        ],
        compiler_params=pltpu.CompilerParams(vmem_limit_bytes=VMEM_LIMIT),
        cost_estimate=pl.CostEstimate(flops=12 << 30, bytes_accessed=8 << 20, transcendentals=0),
        name="spectra_and_contract",
    )(column, fields, basis, legendre)


def contract_rest(plan, table, column, legendre):
    lats = legendre.shape[0]
    return pl.pallas_call(
        functools.partial(contract_kernel, plan),
        grid_spec=pltpu.PrefetchScalarGridSpec(
            num_scalar_prefetch=1,
            grid=(plan.steps,),
            in_specs=[
                pl.BlockSpec(table.shape, lambda i, c: (0, 0)),
                pl.BlockSpec((lats, plan.width), lambda i, c: (0, plan.block(i))),
            ],
            out_specs=pl.BlockSpec(plan.shape, lambda i, c: (0, 0, 0)),
            scratch_shapes=contract_scratch(plan),
        ),
        out_shape=jax.ShapeDtypeStruct(plan.shape, BF16),
        compiler_params=pltpu.CompilerParams(vmem_limit_bytes=VMEM_LIMIT),
        cost_estimate=pl.CostEstimate(flops=8 << 30, bytes_accessed=8 << 20, transcendentals=0),
        name="contract_rest",
    )(column, table, legendre)


def split(value, pieces):
    out = []
    for _ in range(pieces):
        piece = value.astype(BF16)
        out.append(piece)
        value = value - piece.astype(F32)
    return out


def panel_kernel(plan, got_ref, lam_ref, w_ref, diag_ref, inverse_ref, slabs_ref, q_ref, g_ref, y_ref, x_ref, z_ref):
    nt = w_ref.shape[0]
    lanes = PANEL + LANE
    plan.gather_sums(got_ref, slabs_ref)
    coef = jnp.concatenate(
        [plan.tile(slabs_ref, plan.first_panel + n) for n in range(plan.panel_tiles)], axis=1
    )
    lam = lam_ref[...]
    scaled = coef / lam
    starts, total = [], 0
    for r in range(nt):
        low = r // 8 * 8
        z_ref[total : total + nt - low, :] = coef[low:, :] * scaled[r : r + 1, :]
        starts.append(total)
        total += nt - low
    ids = lax.broadcasted_iota(jnp.int32, (PANEL, lanes), 0)
    upto = lax.broadcasted_iota(jnp.int32, (PANEL, lanes), 1)
    tri = jnp.where(ids < upto, 1.0, 0.0).astype(BF16)
    prefix = 0.0
    for piece in split(z_ref[...], 3)[::-1]:
        prefix = prefix + jnp.dot(piece, tri, preferred_element_type=F32)
    q_ref[...] = prefix
    y_ref[:, :PANEL] = coef
    eye = lax.broadcasted_iota(jnp.int32, (nt, LANE), 0) == lax.broadcasted_iota(jnp.int32, (nt, LANE), 1)
    y_ref[:, PANEL:] = jnp.where(eye, 1.0, 0.0)
    inverses = []
    for r in range(nt):
        low = r // 8 * 8
        place = low + lax.broadcasted_iota(jnp.int32, (nt - low, lanes), 0)
        row = q_ref[starts[r] : starts[r] + nt - low, :] + jnp.where(place == r, float(nt), 0.0)
        for p in range(r):
            base = starts[p] + low - p // 8 * 8
            factor = g_ref[starts[p] + r - p // 8 * 8 : starts[p] + r - p // 8 * 8 + 1, :]
            row = row - factor * q_ref[base : base + nt - low, :]
        q_ref[starts[r] : starts[r] + nt - low, :] = row
        inv = 1.0 / row[r - low : r - low + 1, :]
        inverses.append(inv)
        ratio = jnp.where(place > r, row * inv, 0.0)
        g_ref[starts[r] : starts[r] + nt - low, :] = ratio
        y_ref[low:, :] = y_ref[low:, :] - ratio * y_ref[r : r + 1, :]
    x_ref[...] = jnp.zeros_like(x_ref)
    for r in range(nt - 1, -1, -1):
        low = r // 8 * 8
        ratio = g_ref[starts[r] : starts[r] + nt - low, :]
        tail = jnp.sum(ratio * x_ref[low:, :], axis=0, keepdims=True)
        x_ref[r : r + 1, :] = y_ref[r : r + 1, :] * inverses[r] - tail
    solved = x_ref[:, :PANEL]
    pivot = jnp.sqrt(lam + jnp.sum(coef * solved, axis=0, keepdims=True))
    w_ref[...] = solved / pivot
    diag_ref[...] = lam / pivot
    inverse_ref[...] = x_ref[:, PANEL:]


def panel_small(plan, got, lam):
    nt = plan.times * plan.tm_count
    rows = sum(nt - r // 8 * 8 for r in range(nt))
    lanes = PANEL + LANE
    return pl.pallas_call(
        functools.partial(panel_kernel, plan),
        grid=(1,),
        in_specs=[
            pl.BlockSpec(plan.shape, lambda i: (0, 0, 0)),
            pl.BlockSpec((1, PANEL), lambda i: (0, 0)),
        ],
        out_specs=[
            pl.BlockSpec((nt, PANEL), lambda i: (0, 0)),
            pl.BlockSpec((1, PANEL), lambda i: (0, 0)),
            pl.BlockSpec((nt, LANE), lambda i: (0, 0)),
        ],
        out_shape=[
            jax.ShapeDtypeStruct((nt, PANEL), F32),
            jax.ShapeDtypeStruct((1, PANEL), F32),
            jax.ShapeDtypeStruct((nt, LANE), F32),
        ],
        scratch_shapes=[
            pltpu.VMEM(plan.sums_shape, F32),
            pltpu.VMEM((rows, lanes), F32),
            pltpu.VMEM((rows, lanes), F32),
            pltpu.VMEM((nt, lanes), F32),
            pltpu.VMEM((nt, lanes), F32),
            pltpu.VMEM((rows, PANEL), F32),
        ],
        compiler_params=pltpu.CompilerParams(vmem_limit_bytes=VMEM_LIMIT),
        cost_estimate=pl.CostEstimate(flops=4 << 30, bytes_accessed=1 << 18, transcendentals=0),
        name="panel_small",
    )(got, lam)


def panel_large(plan, got, lam):
    low = plan.first_panel * LANE
    coef, lam = plan.unpack(got)[:, low : low + PANEL], lam[:, :PANEL]
    nt = coef.shape[0]
    gram = jnp.dot(coef.T, coef, precision=lax.Precision.HIGHEST) / nt + jnp.diag(lam[0])
    factor = jnp.linalg.cholesky(gram)
    solved = jax.scipy.linalg.solve_triangular(factor, coef.T, lower=True)
    w = solved.T / nt
    rest = jnp.eye(nt, dtype=F32) / nt - jnp.dot(w, w.T, precision=lax.Precision.HIGHEST)
    pivot = jnp.diagonal(factor)[None, :]
    pad = -(-nt // LANE) * LANE - nt
    return w, pivot - jnp.sum(coef * w, axis=0, keepdims=True), jnp.pad(rest, ((0, 0), (0, pad)))


def stack_pieces(value):
    high, low = split(value, 2)
    return jnp.concatenate([high.astype(F32), low.astype(F32)], axis=0).astype(BF16)


def twice(value):
    return jnp.concatenate([value, value], axis=0).astype(BF16)


def contract_times(left, right):
    return lax.dot_general(left, right, (((0,), (0,)), ((), ())), preferred_element_type=F32)


def times_first(value):
    return value.astype(F32).T.astype(BF16)


def tile_kernel(early, late, first_ref, second_ref, w_ref, diag_ref, lam_ref, inverse_ref, out_ref,
                first_slabs, second_slabs, rows_ref, cols_ref, left_ref, left_panel_ref):
    height, width = out_ref.shape
    nt = rows_ref.shape[0]
    step = pl.program_id(0)
    tm_index = lax.axis_index("tm")
    row_start = tm_index * height
    col_start = lax.axis_index("lat") * cols_ref.shape[1] + step * width
    in_panel_rows = row_start < PANEL
    in_panel_cols = col_start < PANEL
    on_diagonal = (row_start < col_start + width) & (col_start < row_start + height)

    @pl.when(step == 0)
    def _():
        early.gather_sums(first_ref, first_slabs)
        late.gather_sums(second_ref, second_slabs)
        for n in range(early.col_tiles):
            cols_ref[:, n * LANE : (n + 1) * LANE] = early.tile(first_slabs, n)
        for n in range(late.col_tiles):
            low = early.take + n * LANE
            cols_ref[:, low : low + LANE] = late.tile(second_slabs, n)
        in_early = early.holds_rows(tm_index)
        for n in range(early.row_tiles):
            value = jnp.where(
                in_early,
                early.tile(first_slabs, early.col_tiles + n),
                late.tile(second_slabs, late.col_tiles + n),
            )
            rows_ref[:, n * LANE : (n + 1) * LANE] = value
        left_ref[...] = times_first(twice(rows_ref[...]))

    @pl.when((step == 0) & in_panel_rows)
    def _():
        low = pl.multiple_of(jnp.minimum(row_start, PANEL - height), LANE)
        left_panel_ref[...] = times_first(stack_pieces(w_ref[:, pl.ds(low, height)]))

    def ids():
        rows = row_start + lax.broadcasted_iota(jnp.int32, (height, width), 0)
        return rows, col_start + lax.broadcasted_iota(jnp.int32, (height, width), 1)

    def product(left, right):
        return jnp.dot(left, right, preferred_element_type=F32)

    own = pl.ds(pl.multiple_of(step * width, LANE), width)

    @pl.when(in_panel_cols & in_panel_rows)
    def _():
        row_ids, col_ids = ids()
        value = product(left_ref[...], stack_pieces(w_ref[...]))
        value = jnp.where(row_ids >= col_ids, value, 0.0)
        out_ref[...] = value + jnp.where(row_ids == col_ids, diag_ref[...], 0.0)

    @pl.when(in_panel_cols & jnp.logical_not(in_panel_rows))
    def _():
        out_ref[...] = product(left_ref[...], stack_pieces(w_ref[...]))

    @pl.when(jnp.logical_not(in_panel_cols) & in_panel_rows)
    def _():
        out_ref[...] = product(left_panel_ref[...], twice(cols_ref[:, own]))

    @pl.when(jnp.logical_not(in_panel_cols) & jnp.logical_not(in_panel_rows))
    def _():
        turned = contract_times(stack_pieces(inverse_ref[:, :nt]), twice(cols_ref[:, own]))
        value = product(left_ref[...], stack_pieces(turned))

        @pl.when(on_diagonal)
        def _():
            row_ids, col_ids = ids()
            lam = lam_ref[:, pl.ds(pl.multiple_of(col_start, LANE), width)]
            out_ref[...] = value + jnp.where(row_ids == col_ids, lam, 0.0)

        @pl.when(jnp.logical_not(on_diagonal))
        def _():
            out_ref[...] = value


def out_tile(early, late, first, second, w, diag, lam, inverse):
    nt, height, width = early.times * early.tm_count, early.rows_width, early.part_width
    whole = lambda i: (0, 0)
    return pl.pallas_call(
        functools.partial(tile_kernel, early, late),
        grid=(width // PANEL,),
        in_specs=[
            pl.BlockSpec(early.shape, lambda i: (0, 0, 0)),
            pl.BlockSpec(late.shape, lambda i: (0, 0, 0)),
            pl.BlockSpec((nt, PANEL), whole),
            pl.BlockSpec((1, PANEL), whole),
            pl.BlockSpec(lam.shape, whole),
            pl.BlockSpec(inverse.shape, whole),
        ],
        out_specs=pl.BlockSpec((height, PANEL), lambda i: (0, i)),
        out_shape=jax.ShapeDtypeStruct((height, width), F32),
        scratch_shapes=[
            pltpu.VMEM(early.sums_shape, F32),
            pltpu.VMEM(late.sums_shape, F32),
            pltpu.VMEM((nt, height), F32),
            pltpu.VMEM((nt, width), F32),
            pltpu.VMEM((height, 2 * nt), BF16),
            pltpu.VMEM((height, 2 * nt), BF16),
        ],
        compiler_params=pltpu.CompilerParams(vmem_limit_bytes=VMEM_LIMIT),
        cost_estimate=pl.CostEstimate(
            flops=4 * nt * height * width, bytes_accessed=4 * height * width, transcendentals=0
        ),
        name="out_tile",
    )(first, second, w, diag, lam, inverse)


def on_device(basis, fields, legendre, order_table, window_start, ridge):
    times, _, nlon = fields.shape
    kcoef = legendre.shape[1]
    tm_count, lat_count = lax.axis_size("tm"), lax.axis_size("lat")
    window = lax.dynamic_slice_in_dim(order_table, window_start[0], kcoef, 1)
    degree = window[0:1]
    column = SUB * (window[1] + nlon // 2 * window[2])
    lam = ridge[0] * (1.0 + (degree * (degree + 1)).astype(F32) / float(LMAX * (LMAX + 1)))
    part_width = kcoef // lat_count
    cut = max(PANEL, part_width // 2)
    early = Plan(kcoef, tm_count, lat_count, times, 0, cut, True)
    late = Plan(kcoef, tm_count, lat_count, times, cut, part_width - cut, False)

    def exchange(sent):
        return lax.all_to_all(sent, ("tm", "lat"), 0, 0, tiled=True)

    sent, table = spectra_and_contract(early, fields, basis, column, legendre)
    first = exchange(sent)
    second = exchange(contract_rest(late, table, column, legendre))
    small = times * tm_count <= LANE // 4
    w, diag, inverse = (panel_small if small else panel_large)(early, first, lam)
    return out_tile(early, late, first, second, w, diag, lam, inverse)


def solution(mesh):
    def run(fields, legendre, order_table, window_start, ridge):
        basis = jnp.asarray(basis_table(fields.shape[2]))
        placed = (P(), P("tm", "lat", None), P("lat", None), P(), P(), P())
        body = jax.shard_map(on_device, mesh=mesh, in_specs=placed, out_specs=P("tm", "lat"), check_vma=False)
        return body(basis, fields, legendre, order_table, window_start, ridge)

    return run
```

time: 84.3 us -> 64.7 us (0.77)
  blocking collectives: 7.03 us -> 0 us
  Pallas kernels: 46.2 us -> 40.3 us
  starting transfers between devices: 15 us -> 11.4 us
  waiting for transfers between devices: 3.19 us -> 6.72 us
  other arithmetic: 6.78 us -> 3.47 us
  local copies, waits for them, and re-layouts: 3.57 us -> 0.75 us
    psum x1 -> x0, blocking collectives: 7.03 us -> none  [on_device(): coef = lax.psum(part, 'lat').astype(BF16)]
    pallas_call x4, Pallas kernels: 46.2 us -> 40.3 us  [the longest x1 15.2 us: spectra_and_contract(): pl.pallas_call(functools.partial(spectra_kernel, plan, 1.0 / math.sqrt(nl...]
    all_to_all x2, starting transfers between devices: 15 us -> 11.4 us  [exchange(): return lax.all_to_all(sent, ('tm', 'lat'), 0, 0, tiled=True)]
    all_to_all x2, waiting for transfers between devices: 3.19 us -> 6.72 us  [exchange(): return lax.all_to_all(sent, ('tm', 'lat'), 0, 0, tiled=True)]
    concatenate x2 -> x0, other arithmetic: 1.83 us -> none  [the longest x1 0.98 us: on_device(): jnp.concatenate([jnp.broadcast_to(cols_own[None], (tm_count, times, cols_...]
    add x1 -> x0, other arithmetic: 1.8 us -> none  [on_device(): column = window[1:2] + nlon // 2 * window[2:3]]
    mul x0 -> x1, other arithmetic: none -> 1.8 us  [on_device(): column = SUB * (window[1] + nlon // 2 * window[2])]
    broadcast_in_dim x2 -> x0, local copies, waits for them, and re-layouts: 1.54 us -> none  [the longest x1 1.34 us: on_device(): jnp.broadcast_to(panel_part[None], (tm_count * lat_count, times, PANEL))]
  transfers between devices with their start and end apart: 2 -> 2, of which waited for: 1 -> 2; matrix products, arithmetic and copies ran while one was open for 7% -> 3% of each run, Pallas kernels for 35% -> 27%
where the time goes in v2:
time: 64.7 us; the launch traced here: 64 us
  Pallas kernels  40.3 us (62%)
  starting transfers between devices  11.4 us (18%)
  waiting for transfers between devices  6.72 us (10%)
  other arithmetic  3.47 us (5%)
  between operations  1.33 us (2%)
  local copies, waits for them, and re-layouts  0.75 us (1%)
    pallas_call x1, Pallas kernels, spectra_and_contract(): pl.pallas_call(functools.partial(spectra_kernel, plan, 1.0 / math.sqrt(nl...  15.2 us
    all_to_all x2, starting transfers between devices, exchange(): return lax.all_to_all(sent, ('tm', 'lat'), 0, 0, tiled=True)  11.4 us
    pallas_call x1, Pallas kernels, contract_rest(): pl.pallas_call(functools.partial(contract_kernel, plan), grid_spec=pltpu....  11 us
    pallas_call x1, Pallas kernels, out_tile(): pl.pallas_call(functools.partial(tile_kernel, early, late), grid=(width /...  7.79 us
    all_to_all x2, waiting for transfers between devices, exchange(): return lax.all_to_all(sent, ('tm', 'lat'), 0, 0, tiled=True)  6.72 us
    pallas_call x1, Pallas kernels, panel_small(): pl.pallas_call(functools.partial(panel_kernel, plan), grid=(1,), in_specs...  6.32 us
    mul x1, other arithmetic, on_device(): column = SUB * (window[1] + nlon // 2 * window[2])  1.8 us
    mul x1, other arithmetic, on_device(): ridge[0]  1.67 us
  transfers between devices with their start and end apart: 2, of which 2 were waited for; matrix products, arithmetic and copies ran while one was open for 3% of the time, Pallas kernels for 27%

profile of v2, /device:TPU:1, one launch (start us, length us, event | category | flops | bytes accessed | tf_op | source)
XLA Modules:
  0.0 64.0 jit_solution(12662899826082191961)
XLA Ops:
  0.7 1.8 %fusion.5 = s32[1,8192]{1,0:T(1,128)} fusion(s32[3,16384]{1,0:T(4,128)} %param.8, s32[]{:T(128)S(6)} %add.26, s32[]{:T(128)S(6)} %select_n.3, s32[]{:T(128)S(6)} %add.25), kind=kLoop, calls=%fused_computation.7 | loop fusion | flops 24576 | bytes 98316 | tf_op jit(solution)/shard_map/mul | solution.py:510
  2.5 15.2 %spectra_and_contract.1 = (bf16[32,16,384]{2,1,0:T(8,128)(2,1)}, f32[11520,128]{1,0:T(8,128)}) custom-call(s32[8192]{0:T(1024)} %bitcast.7, bf16[2,360,1440]{2,1,0:T(8,128)(2,1)} %fields_ref.1, bf16[1440,1440]{1,0:T(8,128)(2,1)} %constant.17.clone.basis_ref, bf16[360,8192]{1,0:T(8,128)(2,1)} %weights_ref.3), custom_call_target="tpu_custom_call" | custom-call | flops 12884901888 | bytes 8388608 | tf_op jit(solution)/shard_map/spectra_and_contract/pallas_call | solution.py:216
  17.6 7.1 %all-to-all-start = ((bf16[32,16,384]{2,1,0:T(8,128)(2,1)}), bf16[32,16,384]{2,1,0:T(8,128)(2,1)S(1)}, u32[]{:S(2)}, u32[]{:S(2)}) async-start(bf16[32,16,384]{2,1,0:T(8,128)(2,1)} %get-tuple-element.10), calls=%async_computation | async-start | bytes 786432 | tf_op jit(solution)/shard_map/all_to_all | solution.py:518
  25.4 11.0 %contract_rest.1 = bf16[32,16,384]{2,1,0:T(8,128)(2,1)} custom-call(s32[8192]{0:T(1024)} %bitcast.8, f32[11520,128]{1,0:T(8,128)} %get-tuple-element.11.table_ref, bf16[360,8192]{1,0:T(8,128)(2,1)} %weights_ref.3), custom_call_target="tpu_custom_call" | custom-call | flops 8589934592 | bytes 8388608 | tf_op jit(solution)/shard_map/contract_rest/pallas_call | solution.py:249
  36.4 1.5 %all-to-all-done.got_ref.first_ref = bf16[32,16,384]{2,1,0:T(8,128)(2,1)S(1)} async-done(((bf16[32,16,384]{2,1,0:T(8,128)(2,1)}), bf16[32,16,384]{2,1,0:T(8,128)(2,1)S(1)}, u32[]{:S(2)}, u32[]{:S(2)}) %all-to-all-start) | async-done | bytes 393248 | tf_op jit(solution)/shard_map/all_to_all | solution.py:518
  37.9 0.0 copy-start
  37.9 4.3 %all-to-all-start.1 = ((bf16[32,16,384]{2,1,0:T(8,128)(2,1)}), bf16[32,16,384]{2,1,0:T(8,128)(2,1)S(1)}, u32[]{:S(2)}, u32[]{:S(2)}) async-start(bf16[32,16,384]{2,1,0:T(8,128)(2,1)} %contract_rest.1), calls=%async_computation.1 | async-start | bytes 786432 | tf_op jit(solution)/shard_map/all_to_all | solution.py:518
  42.3 1.7 %fusion.3.lam_ref = f32[1,8192]{1,0:T(1,128)} fusion(s32[3,16384]{1,0:T(4,128)} %param.8, s32[]{:T(128)S(6)} %select_n.3, f32[]{:T(128)} %bitcast.6), kind=kLoop, calls=%fused_computation.4 | loop fusion | flops 49152 | bytes 65544 | tf_op jit(solution)/shard_map/mul | solution.py:511
  43.9 0.0 copy-done
  44.0 6.3 %panel_small.1 = (f32[32,512]{1,0:T(8,128)}, f32[1,512]{1,0:T(1,128)}, f32[32,128]{1,0:T(8,128)}) custom-call(bf16[32,16,384]{2,1,0:T(8,128)(2,1)} %copy-done, f32[1,8192]{1,0:T(1,128)} %fusion.3.lam_ref), custom_call_target="tpu_custom_call" | custom-call | flops 4294967296 | bytes 262144 | tf_op jit(solution)/shard_map/panel_small/pallas_call | solution.py:334
  50.3 5.2 %all-to-all-done.1.second_ref = bf16[32,16,384]{2,1,0:T(8,128)(2,1)S(1)} async-done(((bf16[32,16,384]{2,1,0:T(8,128)(2,1)}), bf16[32,16,384]{2,1,0:T(8,128)(2,1)S(1)}, u32[]{:S(2)}, u32[]{:S(2)}) %all-to-all-start.1) | async-done | bytes 393248 | tf_op jit(solution)/shard_map/all_to_all | solution.py:518
  55.5 0.0 copy-start.1
  55.5 0.7 %copy-done.1 = bf16[32,16,384]{2,1,0:T(8,128)(2,1)} copy-done((bf16[32,16,384]{2,1,0:T(8,128)(2,1)}, bf16[32,16,384]{2,1,0:T(8,128)(2,1)S(1)}, u32[]{:S(2)}) %copy-start.1) | copy-done | bytes 393240
  56.2 7.8 %out_tile.1 = f32[512,4096]{1,0:T(8,128)} custom-call(bf16[32,16,384]{2,1,0:T(8,128)(2,1)} %copy-done, bf16[32,16,384]{2,1,0:T(8,128)(2,1)} %copy-done.1, f32[32,512]{1,0:T(8,128)} %get-tuple-element.12.w_ref, f32[1,512]{1,0:T(1,128)} %get-tuple-element.13.diag_ref, f32[1,8192]{1,0:T(1,128)} %fusion.3.lam_ref, f32[32,128]{1,0:T(8,128)} %get-tuple-element.14.inverse_ref), custom_call_target="tpu_custom_call" | custom-call | flops 268435456 | bytes 8388608 | tf_op jit(solution)/shard_map/out_tile/pallas_call | solution.py:475
Async XLA Ops:
  17.6 20.3 %all-to-all-start = ((bf16[32,16,384]{2,1,0:T(8,128)(2,1)}), bf16[32,16,384]{2,1,0:T(8,128)(2,1)S(1)}, u32[]{:S(2)}, u32[]{:S(2)}) async-start(bf16[32,16,384]{2,1,0:T(8,128)(2,1)} %get-tuple-element.10), calls=%async_computation | async-start | bytes 786432 | tf_op jit(solution)/shard_map/all_to_all | solution.py:518
  37.9 6.0 %copy-start = (bf16[32,16,384]{2,1,0:T(8,128)(2,1)}, bf16[32,16,384]{2,1,0:T(8,128)(2,1)S(1)}, u32[]{:S(2)}) copy-start(bf16[32,16,384]{2,1,0:T(8,128)(2,1)S(1)} %all-to-all-done.got_ref.first_ref) | copy-start | bytes 1179652
  37.9 17.5 %all-to-all-start.1 = ((bf16[32,16,384]{2,1,0:T(8,128)(2,1)}), bf16[32,16,384]{2,1,0:T(8,128)(2,1)S(1)}, u32[]{:S(2)}, u32[]{:S(2)}) async-start(bf16[32,16,384]{2,1,0:T(8,128)(2,1)} %contract_rest.1), calls=%async_computation.1 | async-start | bytes 786432 | tf_op jit(solution)/shard_map/all_to_all | solution.py:518
  55.5 0.7 %copy-start.1 = (bf16[32,16,384]{2,1,0:T(8,128)(2,1)}, bf16[32,16,384]{2,1,0:T(8,128)(2,1)S(1)}, u32[]{:S(2)}) copy-start(bf16[32,16,384]{2,1,0:T(8,128)(2,1)S(1)} %all-to-all-done.1.second_ref) | copy-start | bytes 1179652

commit v3 on v2

v3 whole, which is shorter than its diff:
```python
import functools
import math

import jax
import jax.numpy as jnp
import ml_dtypes
import numpy as np
from jax import lax
from jax.experimental import pallas as pl
from jax.experimental.pallas import tpu as pltpu
from jax.sharding import PartitionSpec as P

LMAX = 720
PANEL = 512
LANE = 128
SUB = 8
GATHER = 256
GROUP = 4
TRANSFORMS = 3
WIDE = 256
SPECTRA_VMEM = 36 * 1024 * 1024
SMALL_VMEM = 20 * 1024 * 1024
F32 = jnp.float32
BF16 = jnp.bfloat16


def basis_table(nlon):
    half = nlon // 2
    column = np.arange(nlon, dtype=np.int64)[:, None]
    longitude = np.arange(nlon, dtype=np.int64)[None, :]
    phase = (column % half * longitude % nlon).astype(np.float32) * np.float32(2.0 * math.pi / nlon)
    return np.where(column < half, np.cos(phase), np.sin(phase)).astype(ml_dtypes.bfloat16)


def pick_rows(column_ref, start, table_ref, picked_ref):
    for j in range(GATHER):
        group = pl.multiple_of(column_ref[start + j], SUB)
        picked_ref[SUB * j : SUB * (j + 1), :] = table_ref[pl.ds(group, SUB), :]


def latitude_sums(picked_ref, weights, times):
    lats = weights.shape[0]
    pieces = -(-lats // LANE)
    picked = [picked_ref[pl.ds(s, GATHER, stride=SUB), :] for s in range(times * pieces)]
    value = jnp.concatenate(
        [jnp.concatenate(picked[pieces * t : pieces * (t + 1)], axis=1) for t in range(times)], axis=0
    )
    spare = jnp.zeros((pieces * LANE - lats, GATHER), BF16)
    every = jnp.dot(value.astype(BF16), jnp.concatenate([weights, spare], axis=0), preferred_element_type=F32)
    shape = (LANE, LANE)
    eye = lax.broadcasted_iota(jnp.int32, shape, 0) == lax.broadcasted_iota(jnp.int32, shape, 1)
    sums = []
    for t in range(times):
        own = []
        for low in range(0, GATHER, LANE):
            square = every[t * GATHER + low : t * GATHER + low + LANE, low : low + LANE]
            own.append(jnp.sum(jnp.where(eye, square, 0.0), axis=0, keepdims=True))
        sums.append(jnp.concatenate(own, axis=1))
    return jnp.concatenate(sums, axis=0)


def contract(plan, column_ref, table_ref, weights_ref, sums_ref, even_ref, odd_ref, weights_copy):
    picked = [even_ref, odd_ref]

    def place(part):
        return jnp.minimum(part, plan.parts - 1) * GATHER

    pick_rows(column_ref, 0, table_ref, even_ref)

    @pl.loop(0, plan.parts // GROUP)
    def _(group):
        weights_copy(group).wait()
        for n in range(GROUP):
            part = group * GROUP + n
            pick_rows(column_ref, place(part + 1), table_ref, picked[(n + 1) % 2])
            at = pl.ds(pl.multiple_of(part * GATHER, GATHER), GATHER)
            sums_ref[:, at] = latitude_sums(picked[n % 2], weights_ref[:, at], plan.times)


class Plan:
    def __init__(self, kcoef, tm_count, lat_count, times):
        self.tm_count, self.lat_count, self.times = tm_count, lat_count, times
        self.kcoef, self.part_width, self.rows_width = kcoef, kcoef // lat_count, kcoef // tm_count
        self.parts = kcoef // GATHER
        self.half = self.part_width // 2
        self.col_tiles, self.row_tiles, self.panel_tiles = self.half // LANE, self.rows_width // LANE, PANEL // LANE
        self.first_panel = self.col_tiles + self.row_tiles
        self.across = -(-(self.first_panel + self.panel_tiles) // SUB)
        self.slab = (times * SUB, self.across * LANE)
        self.shape = (tm_count * lat_count,) + self.slab
        self.sums_shape = (self.across, tm_count * self.slab[0], LANE)

    def weights_copies(self, legendre_ref, weights_ref, sems):
        width = GROUP * GATHER

        def copy(group):
            own = pl.ds(pl.multiple_of(group * width, width), width)
            return pltpu.make_async_copy(legendre_ref.at[:, own], weights_ref.at[:, own], sems.at[group])

        @pl.loop(0, self.parts // GROUP)
        def _(group):
            copy(group).start()

        return copy

    def spot(self, tile, time):
        low = tile % self.across * LANE
        return time * SUB + tile // self.across, slice(low, low + LANE)

    def pack(self, sums_ref, slab_ref, sent_ref):
        def fill(tile, source, count):
            for n in range(count):
                for t in range(self.times):
                    row, lanes = self.spot(tile + n, t)
                    low = source + n * LANE
                    slab_ref[row : row + 1, lanes] = sums_ref[t : t + 1, low : low + LANE]

        slab_ref[...] = jnp.zeros_like(slab_ref)
        fill(self.first_panel, 0, self.panel_tiles)
        for part in range(self.lat_count):
            for core in range(2):
                fill(0, part * self.part_width + core * self.half, self.col_tiles)
                for owner in range(core, self.tm_count, 2):
                    fill(self.col_tiles, owner * self.rows_width, self.row_tiles)
                    sent_ref[owner * self.lat_count + part] = slab_ref[...].astype(BF16)

    def gather_sums(self, got_ref, slabs_ref):
        rows = self.slab[0]
        for sender in range(self.tm_count):
            first = sender * self.lat_count
            total = got_ref[first].astype(F32)
            for part in range(1, self.lat_count):
                total = total + got_ref[first + part].astype(F32)
            for n in range(self.across):
                slabs_ref[n, sender * rows : (sender + 1) * rows, :] = total[:, n * LANE : (n + 1) * LANE]

    def tile(self, slabs_ref, tile):
        pieces = []
        for t in range(self.times):
            row = t * SUB + tile // self.across
            pieces.append(slabs_ref[tile % self.across, pl.ds(row, self.tm_count, stride=self.slab[0]), :])
        return jnp.concatenate(pieces, axis=0).astype(BF16).astype(F32)

    def unpack(self, got):
        split_shape = (self.tm_count, self.lat_count, self.times, SUB * self.across * LANE)
        total = got.astype(F32).reshape(split_shape).sum(axis=1).astype(BF16).astype(F32)
        return total.transpose(1, 0, 2).reshape(self.times * self.tm_count, -1)


def spectra_kernel(plan, scale, column_ref, fields_ref, basis_ref, legendre_ref, sent_ref,
                   table_ref, fields_buf, basis_buf, weights_ref, lines_ref, even_ref, odd_ref, sums_ref, slab_ref,
                   fields_sem, basis_sem, weights_sem):
    times, lats, nlon = fields_ref.shape
    pieces = -(-lats // LANE)
    rows = nlon // TRANSFORMS
    fields_copy = pltpu.make_async_copy(fields_ref, fields_buf, fields_sem)
    fields_copy.start()
    basis_copies = []
    for step in range(TRANSFORMS):
        part = pl.ds(step * rows, rows)
        copy = pltpu.make_async_copy(basis_ref.at[part, :], basis_buf.at[part, :], basis_sem.at[step])
        copy.start()
        basis_copies.append(copy)
    weights_copy = plan.weights_copies(legendre_ref, weights_ref, weights_sem)
    lines_ref[...] = jnp.zeros_like(lines_ref)
    fields_copy.wait()
    for t in range(times):
        lines_ref[pieces * LANE * t : pieces * LANE * t + lats, :] = fields_buf[t]
    for step in range(TRANSFORMS):
        basis_copies[step].wait()
        spectra = scale * lax.dot_general(
            basis_buf[step * rows : (step + 1) * rows, :], lines_ref[...], (((1,), (1,)), ((), ())),
            preferred_element_type=F32,
        )
        for s in range(times * pieces):
            table_ref[pl.ds(step * rows * SUB + s, rows, stride=SUB), :] = spectra[:, LANE * s : LANE * (s + 1)]
    contract(plan, column_ref, table_ref, weights_ref, sums_ref, even_ref, odd_ref, weights_copy)
    plan.pack(sums_ref, slab_ref, sent_ref)


def in_hbm(value):
    return pltpu.with_memory_space_constraint(value, pltpu.HBM)


def spot_in(space):
    return pl.BlockSpec(memory_space=space)


def spectra_and_contract(plan, fields, basis, column, legendre):
    times, lats, nlon = fields.shape
    pieces = -(-lats // LANE)
    return pl.pallas_call(
        functools.partial(spectra_kernel, plan, 1.0 / math.sqrt(nlon)),
        in_specs=[spot_in(pltpu.SMEM), spot_in(pltpu.HBM), spot_in(pltpu.HBM), spot_in(pltpu.HBM)],
        out_specs=spot_in(pltpu.VMEM),
        out_shape=jax.ShapeDtypeStruct(plan.shape, BF16),
        scratch_shapes=[
            pltpu.VMEM((nlon * SUB, LANE), F32),
            pltpu.VMEM(fields.shape, BF16),
            pltpu.VMEM(basis.shape, BF16),
            pltpu.VMEM((lats, plan.kcoef), BF16),
            pltpu.VMEM((times * pieces * LANE, nlon), BF16),
            pltpu.VMEM((GATHER * SUB, LANE), F32),
            pltpu.VMEM((GATHER * SUB, LANE), F32),
            pltpu.VMEM((times, plan.kcoef), F32),
            pltpu.VMEM(plan.slab, F32),
            pltpu.SemaphoreType.DMA(()),
            pltpu.SemaphoreType.DMA((TRANSFORMS,)),
            pltpu.SemaphoreType.DMA((plan.parts // GROUP,)),
        ],
        compiler_params=pltpu.CompilerParams(vmem_limit_bytes=SPECTRA_VMEM),
        cost_estimate=pl.CostEstimate(flops=12 << 30, bytes_accessed=8 << 20, transcendentals=0),
        name="spectra_and_contract",
    )(column, in_hbm(fields), in_hbm(basis), in_hbm(legendre))


def split(value, pieces):
    out = []
    for _ in range(pieces):
        piece = value.astype(BF16)
        out.append(piece)
        value = value - piece.astype(F32)
    return out


def panel_kernel(plan, got_ref, lam_ref, w_ref, diag_ref, inverse_ref, slabs_ref, q_ref, g_ref, y_ref, x_ref, z_ref):
    nt = w_ref.shape[0]
    lanes = PANEL + LANE
    plan.gather_sums(got_ref, slabs_ref)
    coef = jnp.concatenate(
        [plan.tile(slabs_ref, plan.first_panel + n) for n in range(plan.panel_tiles)], axis=1
    )
    lam = lam_ref[...]
    scaled = coef / lam
    starts, total = [], 0
    for r in range(nt):
        low = r // 8 * 8
        z_ref[total : total + nt - low, :] = coef[low:, :] * scaled[r : r + 1, :]
        starts.append(total)
        total += nt - low
    ids = lax.broadcasted_iota(jnp.int32, (PANEL, lanes), 0)
    upto = lax.broadcasted_iota(jnp.int32, (PANEL, lanes), 1)
    tri = jnp.where(ids < upto, 1.0, 0.0).astype(BF16)
    prefix = 0.0
    for piece in split(z_ref[...], 3)[::-1]:
        prefix = prefix + jnp.dot(piece, tri, preferred_element_type=F32)
    q_ref[...] = prefix
    y_ref[:, :PANEL] = coef
    eye = lax.broadcasted_iota(jnp.int32, (nt, LANE), 0) == lax.broadcasted_iota(jnp.int32, (nt, LANE), 1)
    y_ref[:, PANEL:] = jnp.where(eye, 1.0, 0.0)
    inverses = []
    for r in range(nt):
        low = r // 8 * 8
        place = low + lax.broadcasted_iota(jnp.int32, (nt - low, lanes), 0)
        row = q_ref[starts[r] : starts[r] + nt - low, :] + jnp.where(place == r, float(nt), 0.0)
        for p in range(r):
            base = starts[p] + low - p // 8 * 8
            factor = g_ref[starts[p] + r - p // 8 * 8 : starts[p] + r - p // 8 * 8 + 1, :]
            row = row - factor * q_ref[base : base + nt - low, :]
        q_ref[starts[r] : starts[r] + nt - low, :] = row
        inv = 1.0 / row[r - low : r - low + 1, :]
        inverses.append(inv)
        ratio = jnp.where(place > r, row * inv, 0.0)
        g_ref[starts[r] : starts[r] + nt - low, :] = ratio
        y_ref[low:, :] = y_ref[low:, :] - ratio * y_ref[r : r + 1, :]
    x_ref[...] = jnp.zeros_like(x_ref)
    for r in range(nt - 1, -1, -1):
        low = r // 8 * 8
        ratio = g_ref[starts[r] : starts[r] + nt - low, :]
        tail = jnp.sum(ratio * x_ref[low:, :], axis=0, keepdims=True)
        x_ref[r : r + 1, :] = y_ref[r : r + 1, :] * inverses[r] - tail
    solved = x_ref[:, :PANEL]
    pivot = jnp.sqrt(lam + jnp.sum(coef * solved, axis=0, keepdims=True))
    w_ref[...] = solved / pivot
    diag_ref[...] = lam / pivot
    inverse_ref[...] = x_ref[:, PANEL:]


def panel_small(plan, got, lam):
    nt = plan.times * plan.tm_count
    rows = sum(nt - r // 8 * 8 for r in range(nt))
    lanes = PANEL + LANE
    return pl.pallas_call(
        functools.partial(panel_kernel, plan),
        grid=(1,),
        in_specs=[
            pl.BlockSpec(plan.shape, lambda i: (0, 0, 0)),
            pl.BlockSpec((1, PANEL), lambda i: (0, 0)),
        ],
        out_specs=[
            pl.BlockSpec((nt, PANEL), lambda i: (0, 0)),
            pl.BlockSpec((1, PANEL), lambda i: (0, 0)),
            pl.BlockSpec((nt, LANE), lambda i: (0, 0)),
        ],
        out_shape=[
            jax.ShapeDtypeStruct((nt, PANEL), F32),
            jax.ShapeDtypeStruct((1, PANEL), F32),
            jax.ShapeDtypeStruct((nt, LANE), F32),
        ],
        scratch_shapes=[
            pltpu.VMEM(plan.sums_shape, F32),
            pltpu.VMEM((rows, lanes), F32),
            pltpu.VMEM((rows, lanes), F32),
            pltpu.VMEM((nt, lanes), F32),
            pltpu.VMEM((nt, lanes), F32),
            pltpu.VMEM((rows, PANEL), F32),
        ],
        compiler_params=pltpu.CompilerParams(vmem_limit_bytes=SMALL_VMEM),
        cost_estimate=pl.CostEstimate(flops=4 << 30, bytes_accessed=1 << 18, transcendentals=0),
        name="panel_small",
    )(got, lam)


def panel_large(plan, got, lam):
    low = plan.first_panel * LANE
    coef, lam = plan.unpack(got)[:, low : low + PANEL], lam[:, :PANEL]
    nt = coef.shape[0]
    gram = jnp.dot(coef.T, coef, precision=lax.Precision.HIGHEST) / nt + jnp.diag(lam[0])
    factor = jnp.linalg.cholesky(gram)
    solved = jax.scipy.linalg.solve_triangular(factor, coef.T, lower=True)
    w = solved.T / nt
    rest = jnp.eye(nt, dtype=F32) / nt - jnp.dot(w, w.T, precision=lax.Precision.HIGHEST)
    pivot = jnp.diagonal(factor)[None, :]
    pad = -(-nt // LANE) * LANE - nt
    return w, pivot - jnp.sum(coef * w, axis=0, keepdims=True), jnp.pad(rest, ((0, 0), (0, pad)))


def stack_pieces(value):
    high, low = split(value, 2)
    return jnp.concatenate([high.astype(F32), low.astype(F32)], axis=0).astype(BF16)


def twice(value):
    return jnp.concatenate([value, value], axis=0).astype(BF16)


def contract_times(left, right):
    return lax.dot_general(left, right, (((0,), (0,)), ((), ())), preferred_element_type=F32)


def times_first(value):
    return value.astype(F32).T.astype(BF16)


def tile_kernel(plan, own_ref, other_ref, w_ref, diag_ref, lam_ref, inverse_ref, out_ref,
                own_slabs, other_slabs, rows_ref, cols_ref, left_ref, left_panel_ref, tiles_ref, out_sem):
    height = out_ref.shape[0]
    nt = rows_ref.shape[0]
    tm_index = lax.axis_index("tm")
    row_start = tm_index * height
    first_col = lax.axis_index("lat") * cols_ref.shape[1]
    in_panel_rows = row_start < PANEL

    for got_ref, slabs_ref, core in (
        (own_ref, own_slabs, lax.rem(tm_index, 2)),
        (other_ref, other_slabs, 1 - lax.rem(tm_index, 2)),
    ):
        plan.gather_sums(got_ref, slabs_ref)
        for n in range(plan.col_tiles):
            low = pl.multiple_of(core * plan.half + n * LANE, LANE)
            cols_ref[:, pl.ds(low, LANE)] = plan.tile(slabs_ref, n)
    for n in range(plan.row_tiles):
        rows_ref[:, n * LANE : (n + 1) * LANE] = plan.tile(own_slabs, plan.col_tiles + n)
    left_ref[...] = times_first(twice(rows_ref[...]))

    @pl.when(in_panel_rows)
    def _():
        low = pl.multiple_of(jnp.minimum(row_start, PANEL - height), LANE)
        left_panel_ref[...] = times_first(stack_pieces(w_ref[:, pl.ds(low, height)]))

    def product(left, right):
        return jnp.dot(left, right, preferred_element_type=F32)

    def copy(step):
        own = pl.ds(pl.multiple_of(step * WIDE, WIDE), WIDE)
        return pltpu.make_async_copy(tiles_ref.at[step], out_ref.at[:, own], out_sem.at[step])

    @pl.loop(0, cols_ref.shape[1] // WIDE)
    def _(step):
        col_start = first_col + step * WIDE
        in_panel_cols = col_start < PANEL
        on_diagonal = (row_start < col_start + WIDE) & (col_start < row_start + height)
        own = pl.ds(pl.multiple_of(step * WIDE, WIDE), WIDE)
        out = tiles_ref.at[step]

        def ids():
            rows = row_start + lax.broadcasted_iota(jnp.int32, (height, WIDE), 0)
            return rows, col_start + lax.broadcasted_iota(jnp.int32, (height, WIDE), 1)

        @pl.when(in_panel_cols)
        def _():
            out[...] = product(left_ref[...], stack_pieces(w_ref[:, own_panel(step)]))

        @pl.when(in_panel_cols & in_panel_rows)
        def _():
            row_ids, col_ids = ids()
            diag = jnp.where(row_ids == col_ids, diag_ref[:, own_panel(step)], 0.0)
            out[...] = jnp.where(row_ids >= col_ids, out[...], 0.0) + diag

        @pl.when(jnp.logical_not(in_panel_cols) & in_panel_rows)
        def _():
            out[...] = product(left_panel_ref[...], twice(cols_ref[:, own]))

        @pl.when(jnp.logical_not(in_panel_cols) & jnp.logical_not(in_panel_rows))
        def _():
            turned = contract_times(stack_pieces(inverse_ref[:, :nt]), twice(cols_ref[:, own]))
            out[...] = product(left_ref[...], stack_pieces(turned))

            @pl.when(on_diagonal)
            def _():
                row_ids, col_ids = ids()
                lam = lam_ref[:, pl.ds(pl.multiple_of(col_start, LANE), WIDE)]
                out[...] += jnp.where(row_ids == col_ids, lam, 0.0)

        copy(step).start()

    @pl.loop(0, cols_ref.shape[1] // WIDE)
    def _(step):
        copy(step).wait()


def own_panel(step):
    return pl.ds(pl.multiple_of(jnp.minimum(step * WIDE, PANEL - WIDE), WIDE), WIDE)


def out_tile(plan, own, other, w, diag, lam, inverse):
    nt, height, width = plan.times * plan.tm_count, plan.rows_width, plan.part_width
    return pl.pallas_call(
        functools.partial(tile_kernel, plan),
        in_specs=[spot_in(pltpu.VMEM)] * 6,
        out_specs=spot_in(pltpu.HBM),
        out_shape=jax.ShapeDtypeStruct((height, width), F32),
        scratch_shapes=[
            pltpu.VMEM(plan.sums_shape, F32),
            pltpu.VMEM(plan.sums_shape, F32),
            pltpu.VMEM((nt, height), F32),
            pltpu.VMEM((nt, width), F32),
            pltpu.VMEM((height, 2 * nt), BF16),
            pltpu.VMEM((height, 2 * nt), BF16),
            pltpu.VMEM((width // WIDE, height, WIDE), F32),
            pltpu.SemaphoreType.DMA((width // WIDE,)),
        ],
        compiler_params=pltpu.CompilerParams(vmem_limit_bytes=SMALL_VMEM),
        cost_estimate=pl.CostEstimate(
            flops=4 * nt * height * width, bytes_accessed=4 * height * width, transcendentals=0
        ),
        name="out_tile",
    )(own, other, w, diag, lam, inverse)


def on_device(basis, fields, legendre, order_table, window_start, ridge):
    times, _, nlon = fields.shape
    kcoef = legendre.shape[1]
    tm_count, lat_count = lax.axis_size("tm"), lax.axis_size("lat")
    window = lax.dynamic_slice_in_dim(order_table, window_start[0], kcoef, 1)
    degree = window[0:1]
    column = SUB * (window[1] + nlon // 2 * window[2])
    lam = ridge[0] * (1.0 + (degree * (degree + 1)).astype(F32) / float(LMAX * (LMAX + 1)))
    plan = Plan(kcoef, tm_count, lat_count, times)
    sent = spectra_and_contract(plan, fields, basis, column, legendre)
    own = lax.all_to_all(sent, ("tm", "lat"), 0, 0, tiled=True)
    other = lax.ppermute(own, "tm", [(i, i ^ 1) for i in range(tm_count)])
    small = times * tm_count <= LANE // 4
    w, diag, inverse = (panel_small if small else panel_large)(plan, own, lam)
    return out_tile(plan, own, other, w, diag, lam, inverse)


def solution(mesh):
    def run(fields, legendre, order_table, window_start, ridge):
        basis = jnp.asarray(basis_table(fields.shape[2]))
        placed = (P(), P("tm", "lat", None), P("lat", None), P(), P(), P())
        body = jax.shard_map(on_device, mesh=mesh, in_specs=placed, out_specs=P("tm", "lat"), check_vma=False)
        return body(basis, fields, legendre, order_table, window_start, ridge)

    return run
```

time: 64.7 us -> 55.4 us (0.86)
  Pallas kernels: 40.3 us -> 32.9 us
  waiting for transfers between devices: 6.72 us -> 11.5 us
  starting transfers between devices: 11.4 us -> 7.12 us
  other arithmetic: 3.47 us -> 2.25 us
  local copies, waits for them, and re-layouts: 0.75 us -> 0 us
    pallas_call x2 -> x1, Pallas kernels: 18.8 us -> 7.52 us  [out_tile(): pl.pallas_call(functools.partial(tile_kernel, plan), in_specs=[spot_in(pl...]
    pallas_call x1, Pallas kernels: 15.2 us -> 20.7 us  [spectra_and_contract(): pl.pallas_call(functools.partial(spectra_kernel, plan, 1.0 / math.sqrt(nl...]
    all_to_all x2 -> x1, waiting for transfers between devices: 6.72 us -> 11.5 us  [on_device(): own = lax.all_to_all(sent, ('tm', 'lat'), 0, 0, tiled=True)]
    all_to_all x2 -> x1, starting transfers between devices: 11.4 us -> 7.11 us  [on_device(): own = lax.all_to_all(sent, ('tm', 'lat'), 0, 0, tiled=True)]
    pallas_call x1, Pallas kernels: 6.32 us -> 4.7 us  [panel_small(): pl.pallas_call(functools.partial(panel_kernel, plan), grid=(1,), in_specs...]
    unnamed x4 -> x0, local copies, waits for them, and re-layouts: 0.75 us -> none
  transfers between devices with their start and end apart: 2 -> 2, of which waited for: 2 -> 1; matrix products, arithmetic and copies ran while one was open for 3% -> 2% of each run, Pallas kernels for 27% -> 9%
where the time goes in v3:
time: 55.4 us; the launch traced here: 55.1 us
  Pallas kernels  32.9 us (59%)
  waiting for transfers between devices  11.5 us (21%)
  starting transfers between devices  7.12 us (13%)
  other arithmetic  2.25 us (4%)
  between operations  1.35 us (2%)
    pallas_call x1, Pallas kernels, spectra_and_contract(): pl.pallas_call(functools.partial(spectra_kernel, plan, 1.0 / math.sqrt(nl...  20.7 us
    all_to_all x1, waiting for transfers between devices, on_device(): own = lax.all_to_all(sent, ('tm', 'lat'), 0, 0, tiled=True)  11.5 us
    pallas_call x1, Pallas kernels, out_tile(): pl.pallas_call(functools.partial(tile_kernel, plan), in_specs=[spot_in(pl...  7.52 us
    all_to_all x1, starting transfers between devices, on_device(): own = lax.all_to_all(sent, ('tm', 'lat'), 0, 0, tiled=True)  7.11 us
    pallas_call x1, Pallas kernels, panel_small(): pl.pallas_call(functools.partial(panel_kernel, plan), grid=(1,), in_specs...  4.7 us
    mul x1, other arithmetic, on_device(): column = SUB * (window[1] + nlon // 2 * window[2])  1.2 us
  transfers between devices with their start and end apart: 2, of which 1 were waited for; matrix products, arithmetic and copies ran while one was open for 2% of the time, Pallas kernels for 9%

profile of v3, /device:TPU:1, one launch (start us, length us, event | category | flops | bytes accessed | tf_op | source)
XLA Modules:
  0.0 55.1 jit_solution(12090047152503494484)
XLA Ops:
  0.7 1.2 %fusion.5 = s32[1,8192]{1,0:T(1,128)S(1)} fusion(s32[3,16384]{1,0:T(4,128)} %param.8, s32[]{:T(128)S(6)} %add.26, s32[]{:T(128)S(6)} %select_n.3, s32[]{:T(128)S(6)} %add.25), kind=kLoop, calls=%fused_computation.7 | loop fusion | flops 24576 | bytes 98316 | tf_op jit(solution)/shard_map/mul | solution.py:457
  1.9 20.7 %spectra_and_contract.1 = bf16[32,16,384]{2,1,0:T(8,128)(2,1)} custom-call(s32[8192]{0:T(1024)S(1)} %bitcast.7, bf16[2,360,1440]{2,1,0:T(8,128)(2,1)} %fields_ref.1, bf16[1440,1440]{1,0:T(8,128)(2,1)} %constant.17.clone.basis_ref, bf16[360,8192]{1,0:T(8,128)(2,1)} %legendre_ref.1), custom_call_target="tpu_custom_call" | custom-call | flops 12884901888 | bytes 8388608 | tf_op jit(solution)/shard_map/spectra_and_contract/pallas_call | solution.py:192
  22.6 7.1 %all-to-all-start = ((bf16[32,16,384]{2,1,0:T(8,128)(2,1)}), bf16[32,16,384]{2,1,0:T(8,128)(2,1)S(1)}, u32[]{:S(2)}, u32[]{:S(2)}) async-start(bf16[32,16,384]{2,1,0:T(8,128)(2,1)} %spectra_and_contract.1), calls=%async_computation | async-start | bytes 786432 | tf_op jit(solution)/shard_map/all_to_all | solution.py:461
  30.4 1.1 %fusion.3.lam_ref = f32[1,8192]{1,0:T(1,128)S(1)} fusion(s32[3,16384]{1,0:T(4,128)} %param.8, s32[]{:T(128)S(6)} %select_n.3, f32[]{:T(128)} %bitcast.6), kind=kLoop, calls=%fused_computation.4 | loop fusion | flops 49152 | bytes 65544 | tf_op jit(solution)/shard_map/mul | solution.py:458
  31.4 11.5 %all-to-all-done.got_ref.own_ref = bf16[32,16,384]{2,1,0:T(8,128)(2,1)S(1)} async-done(((bf16[32,16,384]{2,1,0:T(8,128)(2,1)}), bf16[32,16,384]{2,1,0:T(8,128)(2,1)S(1)}, u32[]{:S(2)}, u32[]{:S(2)}) %all-to-all-start) | async-done | bytes 393248 | tf_op jit(solution)/shard_map/all_to_all | solution.py:461
  42.9 0.0 collective-permute-start
  42.9 4.7 %panel_small.1 = (f32[32,512]{1,0:T(8,128)S(1)}, f32[1,512]{1,0:T(1,128)S(1)}, f32[32,128]{1,0:T(8,128)S(1)}) custom-call(bf16[32,16,384]{2,1,0:T(8,128)(2,1)S(1)} %all-to-all-done.got_ref.own_ref, f32[1,8192]{1,0:T(1,128)S(1)} %fusion.3.lam_ref), custom_call_target="tpu_custom_call" | custom-call | flops 4294967296 | bytes 262144 | tf_op jit(solution)/shard_map/panel_small/pallas_call | solution.py:283
  47.6 0.0 collective-permute-done.other_ref
  47.6 7.5 %out_tile.1 = f32[512,4096]{1,0:T(8,128)} custom-call(bf16[32,16,384]{2,1,0:T(8,128)(2,1)S(1)} %all-to-all-done.got_ref.own_ref, bf16[32,16,384]{2,1,0:T(8,128)(2,1)S(1)} %collective-permute-done.other_ref, f32[32,512]{1,0:T(8,128)S(1)} %get-tuple-element.8.w_ref, f32[1,512]{1,0:T(1,128)S(1)} %get-tuple-element.9.diag_ref, f32[1,8192]{1,0:T(1,128)S(1)} %fusion.3.lam_ref, ...), custom_call_target="tpu_custom_call" | custom-call | flops 268435456 | bytes 8388608 | tf_op jit(solution)/shard_map/out_tile/pallas_call | solution.py:428
Async XLA Ops:
  22.6 20.3 %all-to-all-start = ((bf16[32,16,384]{2,1,0:T(8,128)(2,1)}), bf16[32,16,384]{2,1,0:T(8,128)(2,1)S(1)}, u32[]{:S(2)}, u32[]{:S(2)}) async-start(bf16[32,16,384]{2,1,0:T(8,128)(2,1)} %spectra_and_contract.1), calls=%async_computation | async-start | bytes 786432 | tf_op jit(solution)/shard_map/all_to_all | solution.py:461
  42.9 4.7 %collective-permute-start = (bf16[32,16,384]{2,1,0:T(8,128)(2,1)S(1)}, bf16[32,16,384]{2,1,0:T(8,128)(2,1)S(1)}, u32[]{:S(2)}, u32[]{:S(2)}) collective-permute-start(bf16[32,16,384]{2,1,0:T(8,128)(2,1)S(1)} %all-to-all-done.got_ref.own_ref), channel_id=1, source_target_pairs={{0,2},{2,0},{4,6},{6,4},{8,10},{10,8},{12,14},{14,12},{16,18},{18,... | collective-permute-start | bytes 1179656 | tf_op jit(solution)/shard_map/ppermute | solution.py:462

commit v4 on v3

--- a/solution.py
+++ b/solution.py
@@ -17,7 +17,7 @@
 GATHER = 256
 GROUP = 4
 TRANSFORMS = 3
-WIDE = 256
+WIDE = 512
 SPECTRA_VMEM = 36 * 1024 * 1024
 SMALL_VMEM = 20 * 1024 * 1024
 F32 = jnp.float32
@@ -33,8 +33,9 @@
 
 
 def pick_rows(column_ref, start, table_ref, picked_ref):
+    row = start // LANE
     for j in range(GATHER):
-        group = pl.multiple_of(column_ref[start + j], SUB)
+        group = pl.multiple_of(column_ref[row + j // LANE, j % LANE], SUB)
         picked_ref[SUB * j : SUB * (j + 1), :] = table_ref[pl.ds(group, SUB), :]
 
 
@@ -147,12 +148,25 @@
         return total.transpose(1, 0, 2).reshape(self.times * self.tm_count, -1)
 
 
-def spectra_kernel(plan, scale, column_ref, fields_ref, basis_ref, legendre_ref, sent_ref,
-                   table_ref, fields_buf, basis_buf, weights_ref, lines_ref, even_ref, odd_ref, sums_ref, slab_ref,
-                   fields_sem, basis_sem, weights_sem):
+def window_of(value, start, length, lines_ref):
+    for n in range(value.shape[1] // LANE):
+        lines_ref[n : n + 1, :] = value[:, n * LANE : (n + 1) * LANE]
+    over = lax.rem(start, LANE)
+    lines_ref[...] = pltpu.roll(lines_ref[...], lax.rem(LANE - over, LANE), 1)
+    first = lines_ref[pl.ds(start // LANE, length // LANE), :]
+    second = lines_ref[pl.ds(start // LANE + 1, length // LANE), :]
+    lane = lax.broadcasted_iota(jnp.int32, first.shape, 1)
+    return jnp.where(lane < LANE - over, first, second)
+
+
+def spectra_kernel(plan, scale, start_ref, ridge_ref, order_ref, fields_ref, basis_ref, legendre_ref, sent_ref,
+                   lam_ref, order_buf, index_ref, window_ref, column_ref, table_ref, fields_buf, basis_buf, weights_ref, lines_ref, even_ref, odd_ref, sums_ref, slab_ref,
+                   order_sem, column_sem, fields_sem, basis_sem, weights_sem):
     times, lats, nlon = fields_ref.shape
     pieces = -(-lats // LANE)
     rows = nlon // TRANSFORMS
+    order_copy = pltpu.make_async_copy(order_ref, order_buf, order_sem)
+    order_copy.start()
     fields_copy = pltpu.make_async_copy(fields_ref, fields_buf, fields_sem)
     fields_copy.start()
     basis_copies = []
@@ -161,19 +175,35 @@
         copy = pltpu.make_async_copy(basis_ref.at[part, :], basis_buf.at[part, :], basis_sem.at[step])
         copy.start()
         basis_copies.append(copy)
-    weights_copy = plan.weights_copies(legendre_ref, weights_ref, weights_sem)
-    lines_ref[...] = jnp.zeros_like(lines_ref)
+    for t in range(times):
+        end = pieces * LANE * (t + 1)
+        low = end - LANE
+        lines_ref[low:end, :] = jnp.zeros((LANE, nlon), BF16)
+    order_copy.wait()
+    start = start_ref[0]
+    column = SUB * (order_buf[1:2, :] + nlon // 2 * order_buf[2:3, :])
+    window_ref[...] = window_of(column, start, plan.kcoef, index_ref)
+    column_copy = pltpu.make_async_copy(window_ref, column_ref, column_sem)
+    column_copy.start()
+    degree = window_of(order_buf[0:1, :], start, plan.kcoef, index_ref)
+    lam = ridge_ref[0] * (1.0 + (degree * (degree + 1)).astype(F32) / float(LMAX * (LMAX + 1)))
+    for n in range(plan.kcoef // LANE):
+        lam_ref[:, n * LANE : (n + 1) * LANE] = lam[n : n + 1, :]
     fields_copy.wait()
     for t in range(times):
         lines_ref[pieces * LANE * t : pieces * LANE * t + lats, :] = fields_buf[t]
+    basis_copies[0].wait()
+    weights_copy = plan.weights_copies(legendre_ref, weights_ref, weights_sem)
     for step in range(TRANSFORMS):
-        basis_copies[step].wait()
+        if step > 0:
+            basis_copies[step].wait()
         spectra = scale * lax.dot_general(
             basis_buf[step * rows : (step + 1) * rows, :], lines_ref[...], (((1,), (1,)), ((), ())),
             preferred_element_type=F32,
         )
         for s in range(times * pieces):
             table_ref[pl.ds(step * rows * SUB + s, rows, stride=SUB), :] = spectra[:, LANE * s : LANE * (s + 1)]
+    column_copy.wait()
     contract(plan, column_ref, table_ref, weights_ref, sums_ref, even_ref, odd_ref, weights_copy)
     plan.pack(sums_ref, slab_ref, sent_ref)
 
@@ -186,15 +216,20 @@
     return pl.BlockSpec(memory_space=space)
 
 
-def spectra_and_contract(plan, fields, basis, column, legendre):
+def spectra_and_contract(plan, start, ridge, order, fields, basis, legendre):
     times, lats, nlon = fields.shape
+    entries = order.shape[1] // LANE
     pieces = -(-lats // LANE)
     return pl.pallas_call(
         functools.partial(spectra_kernel, plan, 1.0 / math.sqrt(nlon)),
-        in_specs=[spot_in(pltpu.SMEM), spot_in(pltpu.HBM), spot_in(pltpu.HBM), spot_in(pltpu.HBM)],
-        out_specs=spot_in(pltpu.VMEM),
-        out_shape=jax.ShapeDtypeStruct(plan.shape, BF16),
+        in_specs=[spot_in(pltpu.SMEM)] * 2 + [spot_in(pltpu.HBM)] * 4,
+        out_specs=[spot_in(pltpu.VMEM)] * 2,
+        out_shape=[jax.ShapeDtypeStruct(plan.shape, BF16), jax.ShapeDtypeStruct((1, plan.kcoef), F32)],
         scratch_shapes=[
+            pltpu.VMEM(order.shape, jnp.int32),
+            pltpu.VMEM((entries + SUB, LANE), jnp.int32),
+            pltpu.VMEM((plan.kcoef // LANE, LANE), jnp.int32),
+            pltpu.SMEM((plan.kcoef // LANE, LANE), jnp.int32),
             pltpu.VMEM((nlon * SUB, LANE), F32),
             pltpu.VMEM(fields.shape, BF16),
             pltpu.VMEM(basis.shape, BF16),
@@ -205,13 +240,15 @@
             pltpu.VMEM((times, plan.kcoef), F32),
             pltpu.VMEM(plan.slab, F32),
             pltpu.SemaphoreType.DMA(()),
+            pltpu.SemaphoreType.DMA(()),
+            pltpu.SemaphoreType.DMA(()),
             pltpu.SemaphoreType.DMA((TRANSFORMS,)),
             pltpu.SemaphoreType.DMA((plan.parts // GROUP,)),
         ],
         compiler_params=pltpu.CompilerParams(vmem_limit_bytes=SPECTRA_VMEM),
         cost_estimate=pl.CostEstimate(flops=12 << 30, bytes_accessed=8 << 20, transcendentals=0),
         name="spectra_and_contract",
-    )(column, in_hbm(fields), in_hbm(basis), in_hbm(legendre))
+    )(start, ridge, in_hbm(order), in_hbm(fields), in_hbm(basis), in_hbm(legendre))
 
 
 def split(value, pieces):
@@ -343,7 +380,7 @@
 
 
 def tile_kernel(plan, own_ref, other_ref, w_ref, diag_ref, lam_ref, inverse_ref, out_ref,
-                own_slabs, other_slabs, rows_ref, cols_ref, left_ref, left_panel_ref, tiles_ref, out_sem):
+                own_slabs, other_slabs, rows_ref, cols_ref, left_ref, left_main_ref, right_ref, tiles_ref, out_sem):
     height = out_ref.shape[0]
     nt = rows_ref.shape[0]
     tm_index = lax.axis_index("tm")
@@ -366,10 +403,18 @@
     @pl.when(in_panel_rows)
     def _():
         low = pl.multiple_of(jnp.minimum(row_start, PANEL - height), LANE)
-        left_panel_ref[...] = times_first(stack_pieces(w_ref[:, pl.ds(low, height)]))
-
-    def product(left, right):
-        return jnp.dot(left, right, preferred_element_type=F32)
+        left_main_ref[...] = times_first(stack_pieces(w_ref[:, pl.ds(low, height)]))
+        right_ref[...] = twice(cols_ref[...])
+
+    @pl.when(jnp.logical_not(in_panel_rows))
+    def _():
+        left_main_ref[...] = left_ref[...]
+        turned = contract_times(stack_pieces(inverse_ref[:, :nt]), twice(cols_ref[...]))
+        right_ref[...] = stack_pieces(turned)
+
+    @pl.when(first_col < PANEL)
+    def _():
+        right_ref[:, :PANEL] = stack_pieces(w_ref[...])
 
     def copy(step):
         own = pl.ds(pl.multiple_of(step * WIDE, WIDE), WIDE)
@@ -389,7 +434,11 @@
 
         @pl.when(in_panel_cols)
         def _():
-            out[...] = product(left_ref[...], stack_pieces(w_ref[:, own_panel(step)]))
+            out[...] = jnp.dot(left_ref[...], right_ref[:, own], preferred_element_type=F32)
+
+        @pl.when(jnp.logical_not(in_panel_cols))
+        def _():
+            out[...] = jnp.dot(left_main_ref[...], right_ref[:, own], preferred_element_type=F32)
 
         @pl.when(in_panel_cols & in_panel_rows)
         def _():
@@ -397,20 +446,11 @@
             diag = jnp.where(row_ids == col_ids, diag_ref[:, own_panel(step)], 0.0)
             out[...] = jnp.where(row_ids >= col_ids, out[...], 0.0) + diag
 
-        @pl.when(jnp.logical_not(in_panel_cols) & in_panel_rows)
+        @pl.when(on_diagonal & jnp.logical_not(in_panel_rows))
         def _():
-            out[...] = product(left_panel_ref[...], twice(cols_ref[:, own]))
-
-        @pl.when(jnp.logical_not(in_panel_cols) & jnp.logical_not(in_panel_rows))
-        def _():
-            turned = contract_times(stack_pieces(inverse_ref[:, :nt]), twice(cols_ref[:, own]))
-            out[...] = product(left_ref[...], stack_pieces(turned))
-
-            @pl.when(on_diagonal)
-            def _():
-                row_ids, col_ids = ids()
-                lam = lam_ref[:, pl.ds(pl.multiple_of(col_start, LANE), WIDE)]
-                out[...] += jnp.where(row_ids == col_ids, lam, 0.0)
+            row_ids, col_ids = ids()
+            lam = lam_ref[:, pl.ds(pl.multiple_of(col_start, LANE), WIDE)]
+            out[...] += jnp.where(row_ids == col_ids, lam, 0.0)
 
         copy(step).start()
 
@@ -437,6 +477,7 @@
             pltpu.VMEM((nt, width), F32),
             pltpu.VMEM((height, 2 * nt), BF16),
             pltpu.VMEM((height, 2 * nt), BF16),
+            pltpu.VMEM((2 * nt, width), BF16),
             pltpu.VMEM((width // WIDE, height, WIDE), F32),
             pltpu.SemaphoreType.DMA((width // WIDE,)),
         ],
@@ -449,15 +490,11 @@
 
 
 def on_device(basis, fields, legendre, order_table, window_start, ridge):
-    times, _, nlon = fields.shape
+    times = fields.shape[0]
     kcoef = legendre.shape[1]
     tm_count, lat_count = lax.axis_size("tm"), lax.axis_size("lat")
-    window = lax.dynamic_slice_in_dim(order_table, window_start[0], kcoef, 1)
-    degree = window[0:1]
-    column = SUB * (window[1] + nlon // 2 * window[2])
-    lam = ridge[0] * (1.0 + (degree * (degree + 1)).astype(F32) / float(LMAX * (LMAX + 1)))
     plan = Plan(kcoef, tm_count, lat_count, times)
-    sent = spectra_and_contract(plan, fields, basis, column, legendre)
+    sent, lam = spectra_and_contract(plan, window_start, ridge, order_table, fields, basis, legendre)
     own = lax.all_to_all(sent, ("tm", "lat"), 0, 0, tiled=True)
     other = lax.ppermute(own, "tm", [(i, i ^ 1) for i in range(tm_count)])
     small = times * tm_count <= LANE // 4

time: 55.4 us -> 50.2 us (0.906)
  blocking collectives: 0 us -> 20.1 us
  waiting for transfers between devices: 11.5 us -> 0.01 us
  starting transfers between devices: 7.12 us -> 0.01 us
  Pallas kernels: 32.9 us -> 28.2 us
  other arithmetic: 2.25 us -> 0 us
    all_to_all x0 -> x1, blocking collectives: none -> 20.1 us  [on_device(): own = lax.all_to_all(sent, ('tm', 'lat'), 0, 0, tiled=True)]
    all_to_all x1 -> x0, waiting for transfers between devices: 11.5 us -> none  [on_device(): own = lax.all_to_all(sent, ('tm', 'lat'), 0, 0, tiled=True)]
    all_to_all x1 -> x0, starting transfers between devices: 7.11 us -> none  [on_device(): own = lax.all_to_all(sent, ('tm', 'lat'), 0, 0, tiled=True)]
    pallas_call x1, Pallas kernels: 7.52 us -> 4.36 us  [out_tile(): pl.pallas_call(functools.partial(tile_kernel, plan), in_specs=[spot_in(pl...]
    mul x2 -> x0, other arithmetic: 2.25 us -> none  [the longest x1 1.2 us: on_device(): column = SUB * (window[1] + nlon // 2 * window[2])]
    pallas_call x1, Pallas kernels: 20.7 us -> 19.1 us  [spectra_and_contract(): pl.pallas_call(functools.partial(spectra_kernel, plan, 1.0 / math.sqrt(nl...]
  transfers between devices with their start and end apart: 2 -> 1, of which waited for: 1 -> 0; matrix products, arithmetic and copies ran while one was open for 2% -> 0% of each run, Pallas kernels for 9% -> 9%
where the time goes in v4:
time: 50.2 us; the launch traced here: 49.6 us
  Pallas kernels  28.2 us (56%)
  blocking collectives  20.1 us (40%)
  between operations  1.32 us (3%)
    all_to_all x1, blocking collectives, on_device(): own = lax.all_to_all(sent, ('tm', 'lat'), 0, 0, tiled=True)  20.1 us
    pallas_call x1, Pallas kernels, spectra_and_contract(): pl.pallas_call(functools.partial(spectra_kernel, plan, 1.0 / math.sqrt(nl...  19.1 us
    pallas_call x1, Pallas kernels, panel_small(): pl.pallas_call(functools.partial(panel_kernel, plan), grid=(1,), in_specs...  4.71 us
    pallas_call x1, Pallas kernels, out_tile(): pl.pallas_call(functools.partial(tile_kernel, plan), in_specs=[spot_in(pl...  4.36 us
  transfers between devices with their start and end apart: 1, of which 0 were waited for; matrix products, arithmetic and copies ran while one was open for 0% of the time, Pallas kernels for 9%

profile of v4, /device:TPU:1, one launch (start us, length us, event | category | flops | bytes accessed | tf_op | source)
XLA Modules:
  0.0 49.6 jit_solution(6704008205483841054)
XLA Ops:
  1.3 19.1 %spectra_and_contract.1 = (bf16[32,16,384]{2,1,0:T(8,128)(2,1)S(1)}, f32[1,8192]{1,0:T(1,128)S(1)}) custom-call(s32[1]{0:T(128)S(6)} %copy.7.start_ref, f32[1]{0:T(128)S(6)} %copy.8.ridge_ref, s32[3,16384]{1,0:T(4,128)} %order_ref.1, bf16[2,360,1440]{2,1,0:T(8,128)(2,1)} %fields_ref.1, bf16[1440,1440]{1,0:T(8,128)(2,1)} %constant.2.clone.basis_ref, ...), custom_call_target="tpu_custom_call" | custom-call | flops 12884901888 | bytes 8388608 | tf_op jit(solution)/shard_map/spectra_and_contract/pallas_call | solution.py:223
  20.4 20.1 %all_to_all.5.got_ref.own_ref = bf16[32,16,384]{2,1,0:T(8,128)(2,1)S(1)} all-to-all(bf16[32,16,384]{2,1,0:T(8,128)(2,1)S(1)} %get-tuple-element.10), channel_id=1, replica_groups=mesh['tm'=16,'lat'=2] {'tm','lat'}, dimensions={0} | all-to-all | bytes 786432 | tf_op jit(solution)/shard_map/all_to_all | solution.py:498
  40.5 0.0 collective-permute-start
  40.5 4.7 %panel_small.1 = (f32[32,512]{1,0:T(8,128)S(1)}, f32[1,512]{1,0:T(1,128)S(1)}, f32[32,128]{1,0:T(8,128)S(1)}) custom-call(bf16[32,16,384]{2,1,0:T(8,128)(2,1)S(1)} %all_to_all.5.got_ref.own_ref, f32[1,8192]{1,0:T(1,128)S(1)} %get-tuple-element.11.lam_ref), custom_call_target="tpu_custom_call" | custom-call | flops 4294967296 | bytes 262144 | tf_op jit(solution)/shard_map/panel_small/pallas_call | solution.py:320
  45.2 0.0 collective-permute-done.other_ref
  45.2 4.4 %out_tile.1 = f32[512,4096]{1,0:T(8,128)} custom-call(bf16[32,16,384]{2,1,0:T(8,128)(2,1)S(1)} %all_to_all.5.got_ref.own_ref, bf16[32,16,384]{2,1,0:T(8,128)(2,1)S(1)} %collective-permute-done.other_ref, f32[32,512]{1,0:T(8,128)S(1)} %get-tuple-element.12.w_ref, f32[1,512]{1,0:T(1,128)S(1)} %get-tuple-element.13.diag_ref, ...), custom_call_target="tpu_custom_call" | custom-call | flops 268435456 | bytes 8388608 | tf_op jit(solution)/shard_map/out_tile/pallas_call | solution.py:468
Async XLA Ops:
  40.5 4.7 %collective-permute-start = (bf16[32,16,384]{2,1,0:T(8,128)(2,1)S(1)}, bf16[32,16,384]{2,1,0:T(8,128)(2,1)S(1)}, u32[]{:S(2)}, u32[]{:S(2)}) collective-permute-start(bf16[32,16,384]{2,1,0:T(8,128)(2,1)S(1)} %all_to_all.5.got_ref.own_ref), channel_id=1, source_target_pairs={{0,2},{2,0},{4,6},{6,4},{8,10},{10,8},{12,14},{14,12},{16,18},{18,... | collective-permute-start | bytes 1179656 | tf_op jit(solution)/shard_map/ppermute | solution.py:499

commit v5 on v4

--- a/solution.py
+++ b/solution.py
@@ -16,7 +16,6 @@
 SUB = 8
 GATHER = 256
 GROUP = 4
-TRANSFORMS = 3
 WIDE = 512
 SPECTRA_VMEM = 36 * 1024 * 1024
 SMALL_VMEM = 20 * 1024 * 1024
@@ -164,17 +163,12 @@
                    order_sem, column_sem, fields_sem, basis_sem, weights_sem):
     times, lats, nlon = fields_ref.shape
     pieces = -(-lats // LANE)
-    rows = nlon // TRANSFORMS
     order_copy = pltpu.make_async_copy(order_ref, order_buf, order_sem)
     order_copy.start()
     fields_copy = pltpu.make_async_copy(fields_ref, fields_buf, fields_sem)
     fields_copy.start()
-    basis_copies = []
-    for step in range(TRANSFORMS):
-        part = pl.ds(step * rows, rows)
-        copy = pltpu.make_async_copy(basis_ref.at[part, :], basis_buf.at[part, :], basis_sem.at[step])
-        copy.start()
-        basis_copies.append(copy)
+    basis_copy = pltpu.make_async_copy(basis_ref, basis_buf, basis_sem)
+    basis_copy.start()
     for t in range(times):
         end = pieces * LANE * (t + 1)
         low = end - LANE
@@ -192,17 +186,17 @@
     fields_copy.wait()
     for t in range(times):
         lines_ref[pieces * LANE * t : pieces * LANE * t + lats, :] = fields_buf[t]
-    basis_copies[0].wait()
+    basis_copy.wait()
     weights_copy = plan.weights_copies(legendre_ref, weights_ref, weights_sem)
-    for step in range(TRANSFORMS):
-        if step > 0:
-            basis_copies[step].wait()
+    tiles = times * pieces
+    wide = 2 if tiles % 2 == 0 else 1
+    for low in range(0, tiles, wide):
         spectra = scale * lax.dot_general(
-            basis_buf[step * rows : (step + 1) * rows, :], lines_ref[...], (((1,), (1,)), ((), ())),
+            basis_buf[...], lines_ref[LANE * low : LANE * (low + wide), :], (((1,), (1,)), ((), ())),
             preferred_element_type=F32,
         )
-        for s in range(times * pieces):
-            table_ref[pl.ds(step * rows * SUB + s, rows, stride=SUB), :] = spectra[:, LANE * s : LANE * (s + 1)]
+        for s in range(wide):
+            table_ref[pl.ds(low + s, nlon, stride=SUB), :] = spectra[:, LANE * s : LANE * (s + 1)]
     column_copy.wait()
     contract(plan, column_ref, table_ref, weights_ref, sums_ref, even_ref, odd_ref, weights_copy)
     plan.pack(sums_ref, slab_ref, sent_ref)
@@ -242,7 +236,7 @@
             pltpu.SemaphoreType.DMA(()),
             pltpu.SemaphoreType.DMA(()),
             pltpu.SemaphoreType.DMA(()),
-            pltpu.SemaphoreType.DMA((TRANSFORMS,)),
+            pltpu.SemaphoreType.DMA(()),
             pltpu.SemaphoreType.DMA((plan.parts // GROUP,)),
         ],
         compiler_params=pltpu.CompilerParams(vmem_limit_bytes=SPECTRA_VMEM),
@@ -275,13 +269,14 @@
         z_ref[total : total + nt - low, :] = coef[low:, :] * scaled[r : r + 1, :]
         starts.append(total)
         total += nt - low
-    ids = lax.broadcasted_iota(jnp.int32, (PANEL, lanes), 0)
-    upto = lax.broadcasted_iota(jnp.int32, (PANEL, lanes), 1)
+    ids = lax.broadcasted_iota(jnp.int32, (PANEL, PANEL), 0)
+    upto = lax.broadcasted_iota(jnp.int32, (PANEL, PANEL), 1)
     tri = jnp.where(ids < upto, 1.0, 0.0).astype(BF16)
     prefix = 0.0
     for piece in split(z_ref[...], 3)[::-1]:
         prefix = prefix + jnp.dot(piece, tri, preferred_element_type=F32)
-    q_ref[...] = prefix
+    q_ref[:, :PANEL] = prefix
+    q_ref[:, PANEL:] = jnp.broadcast_to(prefix[:, PANEL - 1 :] + z_ref[:, PANEL - 1 :], (total, LANE))
     y_ref[:, :PANEL] = coef
     eye = lax.broadcasted_iota(jnp.int32, (nt, LANE), 0) == lax.broadcasted_iota(jnp.int32, (nt, LANE), 1)
     y_ref[:, PANEL:] = jnp.where(eye, 1.0, 0.0)

time: 50.2 us -> 48.7 us (0.970)
  Pallas kernels: 28.2 us -> 26.7 us
    pallas_call x1, Pallas kernels: 19.1 us -> 18.3 us  [spectra_and_contract(): pl.pallas_call(functools.partial(spectra_kernel, plan, 1.0 / math.sqrt(nl...]
    pallas_call x1, Pallas kernels: 4.71 us -> 4.03 us  [panel_small(): pl.pallas_call(functools.partial(panel_kernel, plan), grid=(1,), in_specs...]
  transfers between devices with their start and end apart: 1 -> 1, of which waited for: 0 -> 0; matrix products, arithmetic and copies ran while one was open for 0% -> 0% of each run, Pallas kernels for 9% -> 8%
where the time goes in v5:
time: 48.7 us; the launch traced here: 48.1 us
  Pallas kernels  26.7 us (55%)
  blocking collectives  20.1 us (41%)
  between operations  1.32 us (3%)
    all_to_all x1, blocking collectives, on_device(): own = lax.all_to_all(sent, ('tm', 'lat'), 0, 0, tiled=True)  20.1 us
    pallas_call x1, Pallas kernels, spectra_and_contract(): pl.pallas_call(functools.partial(spectra_kernel, plan, 1.0 / math.sqrt(nl...  18.3 us
    pallas_call x1, Pallas kernels, out_tile(): pl.pallas_call(functools.partial(tile_kernel, plan), in_specs=[spot_in(pl...  4.36 us
    pallas_call x1, Pallas kernels, panel_small(): pl.pallas_call(functools.partial(panel_kernel, plan), grid=(1,), in_specs...  4.03 us
  transfers between devices with their start and end apart: 1, of which 0 were waited for; matrix products, arithmetic and copies ran while one was open for 0% of the time, Pallas kernels for 8%

profile of v5, /device:TPU:1, one launch (start us, length us, event | category | flops | bytes accessed | tf_op | source)
XLA Modules:
  0.0 48.1 jit_solution(875036994503021110)
XLA Ops:
  1.3 18.3 %spectra_and_contract.1 = (bf16[32,16,384]{2,1,0:T(8,128)(2,1)S(1)}, f32[1,8192]{1,0:T(1,128)S(1)}) custom-call(s32[1]{0:T(128)S(6)} %copy.7.start_ref, f32[1]{0:T(128)S(6)} %copy.8.ridge_ref, s32[3,16384]{1,0:T(4,128)} %order_ref.1, bf16[2,360,1440]{2,1,0:T(8,128)(2,1)} %fields_ref.1, bf16[1440,1440]{1,0:T(8,128)(2,1)} %constant.2.clone.basis_ref, ...), custom_call_target="tpu_custom_call" | custom-call | flops 12884901888 | bytes 8388608 | tf_op jit(solution)/shard_map/spectra_and_contract/pallas_call | solution.py:217
  19.6 20.1 %all_to_all.5.got_ref.own_ref = bf16[32,16,384]{2,1,0:T(8,128)(2,1)S(1)} all-to-all(bf16[32,16,384]{2,1,0:T(8,128)(2,1)S(1)} %get-tuple-element.10), channel_id=1, replica_groups=mesh['tm'=16,'lat'=2] {'tm','lat'}, dimensions={0} | all-to-all | bytes 786432 | tf_op jit(solution)/shard_map/all_to_all | solution.py:493
  39.7 0.0 collective-permute-start
  39.7 4.0 %panel_small.1 = (f32[32,512]{1,0:T(8,128)S(1)}, f32[1,512]{1,0:T(1,128)S(1)}, f32[32,128]{1,0:T(8,128)S(1)}) custom-call(bf16[32,16,384]{2,1,0:T(8,128)(2,1)S(1)} %all_to_all.5.got_ref.own_ref, f32[1,8192]{1,0:T(1,128)S(1)} %get-tuple-element.11.lam_ref), custom_call_target="tpu_custom_call" | custom-call | flops 4294967296 | bytes 262144 | tf_op jit(solution)/shard_map/panel_small/pallas_call | solution.py:315
  43.8 0.0 collective-permute-done.other_ref
  43.8 4.4 %out_tile.1 = f32[512,4096]{1,0:T(8,128)} custom-call(bf16[32,16,384]{2,1,0:T(8,128)(2,1)S(1)} %all_to_all.5.got_ref.own_ref, bf16[32,16,384]{2,1,0:T(8,128)(2,1)S(1)} %collective-permute-done.other_ref, f32[32,512]{1,0:T(8,128)S(1)} %get-tuple-element.12.w_ref, f32[1,512]{1,0:T(1,128)S(1)} %get-tuple-element.13.diag_ref, ...), custom_call_target="tpu_custom_call" | custom-call | flops 268435456 | bytes 8388608 | tf_op jit(solution)/shard_map/out_tile/pallas_call | solution.py:463
Async XLA Ops:
  39.7 4.0 %collective-permute-start = (bf16[32,16,384]{2,1,0:T(8,128)(2,1)S(1)}, bf16[32,16,384]{2,1,0:T(8,128)(2,1)S(1)}, u32[]{:S(2)}, u32[]{:S(2)}) collective-permute-start(bf16[32,16,384]{2,1,0:T(8,128)(2,1)S(1)} %all_to_all.5.got_ref.own_ref), channel_id=1, source_target_pairs={{0,2},{2,0},{4,6},{6,4},{8,10},{10,8},{12,14},{14,12},{16,18},{18,... | collective-permute-start | bytes 1179656 | tf_op jit(solution)/shard_map/ppermute | solution.py:494

commit v6 on v5

--- a/solution.py
+++ b/solution.py
@@ -25,10 +25,15 @@
 
 def basis_table(nlon):
     half = nlon // 2
-    column = np.arange(nlon, dtype=np.int64)[:, None]
-    longitude = np.arange(nlon, dtype=np.int64)[None, :]
-    phase = (column % half * longitude % nlon).astype(np.float32) * np.float32(2.0 * math.pi / nlon)
-    return np.where(column < half, np.cos(phase), np.sin(phase)).astype(ml_dtypes.bfloat16)
+    order = np.concatenate([np.arange(0, half, 2), np.arange(0, half, 2), np.arange(1, half, 2), np.arange(1, half, 2)])
+    sine = np.repeat([False, True, False, True], [half // 2] * 4)[:, None]
+    longitude = np.arange(half, dtype=np.int64)[None, :]
+    phase = (order[:, None] * longitude % nlon).astype(np.float32) * np.float32(2.0 * math.pi / nlon)
+    return np.where(sine, np.sin(phase), np.cos(phase)).astype(ml_dtypes.bfloat16)
+
+
+def basis_row(order, part, nlon):
+    return nlon // 2 * (order & 1) + nlon // 4 * part + (order >> 1)
 
 
 def pick_rows(column_ref, start, table_ref, picked_ref):
@@ -139,11 +144,11 @@
         for t in range(self.times):
             row = t * SUB + tile // self.across
             pieces.append(slabs_ref[tile % self.across, pl.ds(row, self.tm_count, stride=self.slab[0]), :])
-        return jnp.concatenate(pieces, axis=0).astype(BF16).astype(F32)
+        return jnp.concatenate(pieces, axis=0)
 
     def unpack(self, got):
         split_shape = (self.tm_count, self.lat_count, self.times, SUB * self.across * LANE)
-        total = got.astype(F32).reshape(split_shape).sum(axis=1).astype(BF16).astype(F32)
+        total = got.astype(F32).reshape(split_shape).sum(axis=1)
         return total.transpose(1, 0, 2).reshape(self.times * self.tm_count, -1)
 
 
@@ -159,8 +164,9 @@
 
 
 def spectra_kernel(plan, scale, start_ref, ridge_ref, order_ref, fields_ref, basis_ref, legendre_ref, sent_ref,
-                   lam_ref, order_buf, index_ref, window_ref, column_ref, table_ref, fields_buf, basis_buf, weights_ref, lines_ref, even_ref, odd_ref, sums_ref, slab_ref,
-                   order_sem, column_sem, fields_sem, basis_sem, weights_sem):
+                   lam_ref, order_buf, index_ref, window_ref, column_ref, table_ref, fields_buf, basis_buf,
+                   weights_ref, even_lines, odd_lines, even_ref, odd_ref, sums_ref, slab_ref, order_sem,
+                   column_sem, fields_sem, basis_sem, weights_sem):
     times, lats, nlon = fields_ref.shape
     pieces = -(-lats // LANE)
     order_copy = pltpu.make_async_copy(order_ref, order_buf, order_sem)
@@ -171,11 +177,11 @@
     basis_copy.start()
     for t in range(times):
         end = pieces * LANE * (t + 1)
-        low = end - LANE
-        lines_ref[low:end, :] = jnp.zeros((LANE, nlon), BF16)
+        for folded in (even_lines, odd_lines):
+            folded[end - LANE : end, :] = jnp.zeros((LANE, nlon // 2), BF16)
     order_copy.wait()
     start = start_ref[0]
-    column = SUB * (order_buf[1:2, :] + nlon // 2 * order_buf[2:3, :])
+    column = SUB * basis_row(order_buf[1:2, :], order_buf[2:3, :], nlon)
     window_ref[...] = window_of(column, start, plan.kcoef, index_ref)
     column_copy = pltpu.make_async_copy(window_ref, column_ref, column_sem)
     column_copy.start()
@@ -185,18 +191,25 @@
         lam_ref[:, n * LANE : (n + 1) * LANE] = lam[n : n + 1, :]
     fields_copy.wait()
     for t in range(times):
-        lines_ref[pieces * LANE * t : pieces * LANE * t + lats, :] = fields_buf[t]
+        first = fields_buf[t, :, : nlon // 2].astype(F32)
+        second = fields_buf[t, :, nlon // 2 :].astype(F32)
+        own = slice(pieces * LANE * t, pieces * LANE * t + lats)
+        even_lines[own, :] = (first + second).astype(BF16)
+        odd_lines[own, :] = (first - second).astype(BF16)
     basis_copy.wait()
     weights_copy = plan.weights_copies(legendre_ref, weights_ref, weights_sem)
     tiles = times * pieces
     wide = 2 if tiles % 2 == 0 else 1
-    for low in range(0, tiles, wide):
-        spectra = scale * lax.dot_general(
-            basis_buf[...], lines_ref[LANE * low : LANE * (low + wide), :], (((1,), (1,)), ((), ())),
-            preferred_element_type=F32,
-        )
-        for s in range(wide):
-            table_ref[pl.ds(low + s, nlon, stride=SUB), :] = spectra[:, LANE * s : LANE * (s + 1)]
+    for parity, folded in enumerate((even_lines, odd_lines)):
+        half = slice(nlon // 2 * parity, nlon // 2 * (parity + 1))
+        for low in range(0, tiles, wide):
+            spectra = scale * lax.dot_general(
+                basis_buf[half, :], folded[LANE * low : LANE * (low + wide), :], (((1,), (1,)), ((), ())),
+                preferred_element_type=F32,
+            )
+            for s in range(wide):
+                at = pl.ds(SUB * half.start + low + s, nlon // 2, stride=SUB)
+                table_ref[at, :] = spectra[:, LANE * s : LANE * (s + 1)]
     column_copy.wait()
     contract(plan, column_ref, table_ref, weights_ref, sums_ref, even_ref, odd_ref, weights_copy)
     plan.pack(sums_ref, slab_ref, sent_ref)
@@ -228,7 +241,8 @@
             pltpu.VMEM(fields.shape, BF16),
             pltpu.VMEM(basis.shape, BF16),
             pltpu.VMEM((lats, plan.kcoef), BF16),
-            pltpu.VMEM((times * pieces * LANE, nlon), BF16),
+            pltpu.VMEM((times * pieces * LANE, nlon // 2), BF16),
+            pltpu.VMEM((times * pieces * LANE, nlon // 2), BF16),
             pltpu.VMEM((GATHER * SUB, LANE), F32),
             pltpu.VMEM((GATHER * SUB, LANE), F32),
             pltpu.VMEM((times, plan.kcoef), F32),
@@ -357,13 +371,14 @@
     return w, pivot - jnp.sum(coef * w, axis=0, keepdims=True), jnp.pad(rest, ((0, 0), (0, pad)))
 
 
-def stack_pieces(value):
-    high, low = split(value, 2)
-    return jnp.concatenate([high.astype(F32), low.astype(F32)], axis=0).astype(BF16)
-
-
-def twice(value):
-    return jnp.concatenate([value, value], axis=0).astype(BF16)
+def stack_left(value):
+    high, low = (piece.astype(F32) for piece in split(value, 2))
+    return jnp.concatenate([high, high, low], axis=0).astype(BF16)
+
+
+def stack_right(value):
+    high, low = (piece.astype(F32) for piece in split(value, 2))
+    return jnp.concatenate([high, low, high], axis=0).astype(BF16)
 
 
 def contract_times(left, right):
@@ -393,23 +408,23 @@
             cols_ref[:, pl.ds(low, LANE)] = plan.tile(slabs_ref, n)
     for n in range(plan.row_tiles):
         rows_ref[:, n * LANE : (n + 1) * LANE] = plan.tile(own_slabs, plan.col_tiles + n)
-    left_ref[...] = times_first(twice(rows_ref[...]))
+    left_ref[...] = times_first(stack_left(rows_ref[...]))
 
     @pl.when(in_panel_rows)
     def _():
         low = pl.multiple_of(jnp.minimum(row_start, PANEL - height), LANE)
-        left_main_ref[...] = times_first(stack_pieces(w_ref[:, pl.ds(low, height)]))
-        right_ref[...] = twice(cols_ref[...])
+        left_main_ref[...] = times_first(stack_left(w_ref[:, pl.ds(low, height)]))
+        right_ref[...] = stack_right(cols_ref[...])
 
     @pl.when(jnp.logical_not(in_panel_rows))
     def _():
         left_main_ref[...] = left_ref[...]
-        turned = contract_times(stack_pieces(inverse_ref[:, :nt]), twice(cols_ref[...]))
-        right_ref[...] = stack_pieces(turned)
+        turned = contract_times(stack_left(inverse_ref[:, :nt]), stack_right(cols_ref[...]))
+        right_ref[...] = stack_right(turned)
 
     @pl.when(first_col < PANEL)
     def _():
-        right_ref[:, :PANEL] = stack_pieces(w_ref[...])
+        right_ref[:, :PANEL] = stack_right(w_ref[...])
 
     def copy(step):
         own = pl.ds(pl.multiple_of(step * WIDE, WIDE), WIDE)
@@ -470,9 +485,9 @@
             pltpu.VMEM(plan.sums_shape, F32),
             pltpu.VMEM((nt, height), F32),
             pltpu.VMEM((nt, width), F32),
-            pltpu.VMEM((height, 2 * nt), BF16),
-            pltpu.VMEM((height, 2 * nt), BF16),
-            pltpu.VMEM((2 * nt, width), BF16),
+            pltpu.VMEM((height, 3 * nt), BF16),
+            pltpu.VMEM((height, 3 * nt), BF16),
+            pltpu.VMEM((3 * nt, width), BF16),
             pltpu.VMEM((width // WIDE, height, WIDE), F32),
             pltpu.SemaphoreType.DMA((width // WIDE,)),
         ],

time: 48.7 us -> 46.5 us (0.955)
  Pallas kernels: 26.7 us -> 24.5 us
    pallas_call x1, Pallas kernels: 18.3 us -> 16 us  [spectra_and_contract(): pl.pallas_call(functools.partial(spectra_kernel, plan, 1.0 / math.sqrt(nl...]
  transfers between devices with their start and end apart: 1 -> 1, of which waited for: 0 -> 0; matrix products, arithmetic and copies ran while one was open for 0% -> 0% of each run, Pallas kernels for 8% -> 9%
where the time goes in v6:
time: 46.5 us; the launch traced here: 45.9 us
  Pallas kernels  24.5 us (53%)
  blocking collectives  20.1 us (43%)
  between operations  1.32 us (3%)
    all_to_all x1, blocking collectives, on_device(): own = lax.all_to_all(sent, ('tm', 'lat'), 0, 0, tiled=True)  20.1 us
    pallas_call x1, Pallas kernels, spectra_and_contract(): pl.pallas_call(functools.partial(spectra_kernel, plan, 1.0 / math.sqrt(nl...  16 us
    pallas_call x1, Pallas kernels, out_tile(): pl.pallas_call(functools.partial(tile_kernel, plan), in_specs=[spot_in(pl...  4.44 us
    pallas_call x1, Pallas kernels, panel_small(): pl.pallas_call(functools.partial(panel_kernel, plan), grid=(1,), in_specs...  4.05 us
  transfers between devices with their start and end apart: 1, of which 0 were waited for; matrix products, arithmetic and copies ran while one was open for 0% of the time, Pallas kernels for 9%

profile of v6, /device:TPU:1, one launch (start us, length us, event | category | flops | bytes accessed | tf_op | source)
XLA Modules:
  0.0 45.9 jit_solution(4504276802320028815)
XLA Ops:
  1.3 16.0 %spectra_and_contract.1 = (bf16[32,16,384]{2,1,0:T(8,128)(2,1)S(1)}, f32[1,8192]{1,0:T(1,128)S(1)}) custom-call(s32[1]{0:T(128)S(6)} %copy.7.start_ref, f32[1]{0:T(128)S(6)} %copy.8.ridge_ref, s32[3,16384]{1,0:T(4,128)} %order_ref.1, bf16[2,360,1440]{2,1,0:T(8,128)(2,1)} %fields_ref.1, bf16[1440,720]{1,0:T(8,128)(2,1)} %constant.2.clone.basis_ref, ...), custom_call_target="tpu_custom_call" | custom-call | flops 12884901888 | bytes 8388608 | tf_op jit(solution)/shard_map/spectra_and_contract/pallas_call | solution.py:230
  17.3 20.1 %all_to_all.5.got_ref.own_ref = bf16[32,16,384]{2,1,0:T(8,128)(2,1)S(1)} all-to-all(bf16[32,16,384]{2,1,0:T(8,128)(2,1)S(1)} %get-tuple-element.10), channel_id=1, replica_groups=mesh['tm'=16,'lat'=2] {'tm','lat'}, dimensions={0} | all-to-all | bytes 786432 | tf_op jit(solution)/shard_map/all_to_all | solution.py:508
  37.4 0.0 collective-permute-start
  37.4 4.0 %panel_small.1 = (f32[32,512]{1,0:T(8,128)S(1)}, f32[1,512]{1,0:T(1,128)S(1)}, f32[32,128]{1,0:T(8,128)S(1)}) custom-call(bf16[32,16,384]{2,1,0:T(8,128)(2,1)S(1)} %all_to_all.5.got_ref.own_ref, f32[1,8192]{1,0:T(1,128)S(1)} %get-tuple-element.11.lam_ref), custom_call_target="tpu_custom_call" | custom-call | flops 4294967296 | bytes 262144 | tf_op jit(solution)/shard_map/panel_small/pallas_call | solution.py:329
  41.5 0.0 collective-permute-done.other_ref
  41.5 4.4 %out_tile.1 = f32[512,4096]{1,0:T(8,128)} custom-call(bf16[32,16,384]{2,1,0:T(8,128)(2,1)S(1)} %all_to_all.5.got_ref.own_ref, bf16[32,16,384]{2,1,0:T(8,128)(2,1)S(1)} %collective-permute-done.other_ref, f32[32,512]{1,0:T(8,128)S(1)} %get-tuple-element.12.w_ref, f32[1,512]{1,0:T(1,128)S(1)} %get-tuple-element.13.diag_ref, ...), custom_call_target="tpu_custom_call" | custom-call | flops 268435456 | bytes 8388608 | tf_op jit(solution)/shard_map/out_tile/pallas_call | solution.py:478
Async XLA Ops:
  37.4 4.1 %collective-permute-start = (bf16[32,16,384]{2,1,0:T(8,128)(2,1)S(1)}, bf16[32,16,384]{2,1,0:T(8,128)(2,1)S(1)}, u32[]{:S(2)}, u32[]{:S(2)}) collective-permute-start(bf16[32,16,384]{2,1,0:T(8,128)(2,1)S(1)} %all_to_all.5.got_ref.own_ref), channel_id=1, source_target_pairs={{0,2},{2,0},{4,6},{6,4},{8,10},{10,8},{12,14},{14,12},{16,18},{18,... | collective-permute-start | bytes 1179656 | tf_op jit(solution)/shard_map/ppermute | solution.py:509

commit v7 on v6

--- a/solution.py
+++ b/solution.py
@@ -178,7 +178,7 @@
     for t in range(times):
         end = pieces * LANE * (t + 1)
         for folded in (even_lines, odd_lines):
-            folded[end - LANE : end, :] = jnp.zeros((LANE, nlon // 2), BF16)
+            folded[:, end - LANE : end, :] = jnp.zeros((2, LANE, nlon // 2), BF16)
     order_copy.wait()
     start = start_ref[0]
     column = SUB * basis_row(order_buf[1:2, :], order_buf[2:3, :], nlon)
@@ -194,8 +194,9 @@
         first = fields_buf[t, :, : nlon // 2].astype(F32)
         second = fields_buf[t, :, nlon // 2 :].astype(F32)
         own = slice(pieces * LANE * t, pieces * LANE * t + lats)
-        even_lines[own, :] = (first + second).astype(BF16)
-        odd_lines[own, :] = (first - second).astype(BF16)
+        for folded, value in ((even_lines, first + second), (odd_lines, first - second)):
+            for n, piece in enumerate(split(value, 2)):
+                folded[n, own, :] = piece
     basis_copy.wait()
     weights_copy = plan.weights_copies(legendre_ref, weights_ref, weights_sem)
     tiles = times * pieces
@@ -203,9 +204,12 @@
     for parity, folded in enumerate((even_lines, odd_lines)):
         half = slice(nlon // 2 * parity, nlon // 2 * (parity + 1))
         for low in range(0, tiles, wide):
-            spectra = scale * lax.dot_general(
-                basis_buf[half, :], folded[LANE * low : LANE * (low + wide), :], (((1,), (1,)), ((), ())),
-                preferred_element_type=F32,
+            spectra = scale * sum(
+                lax.dot_general(
+                    basis_buf[half, :], folded[n, LANE * low : LANE * (low + wide), :], (((1,), (1,)), ((), ())),
+                    preferred_element_type=F32,
+                )
+                for n in range(2)
             )
             for s in range(wide):
                 at = pl.ds(SUB * half.start + low + s, nlon // 2, stride=SUB)
@@ -241,8 +245,8 @@
             pltpu.VMEM(fields.shape, BF16),
             pltpu.VMEM(basis.shape, BF16),
             pltpu.VMEM((lats, plan.kcoef), BF16),
-            pltpu.VMEM((times * pieces * LANE, nlon // 2), BF16),
-            pltpu.VMEM((times * pieces * LANE, nlon // 2), BF16),
+            pltpu.VMEM((2, times * pieces * LANE, nlon // 2), BF16),
+            pltpu.VMEM((2, times * pieces * LANE, nlon // 2), BF16),
             pltpu.VMEM((GATHER * SUB, LANE), F32),
             pltpu.VMEM((GATHER * SUB, LANE), F32),
             pltpu.VMEM((times, plan.kcoef), F32),

time: 46.5 us -> 48.7 us (1.047)
  Pallas kernels: 24.5 us -> 26.7 us
    pallas_call x1, Pallas kernels: 16 us -> 18.2 us  [spectra_and_contract(): pl.pallas_call(functools.partial(spectra_kernel, plan, 1.0 / math.sqrt(nl...]
  transfers between devices with their start and end apart: 1 -> 1, of which waited for: 0 -> 0; matrix products, arithmetic and copies ran while one was open for 0% -> 0% of each run, Pallas kernels for 9% -> 8%
where the time goes in v7:
time: 48.7 us; the launch traced here: 48.1 us
  Pallas kernels  26.7 us (55%)
  blocking collectives  20.1 us (41%)
  between operations  1.32 us (3%)
    all_to_all x1, blocking collectives, on_device(): own = lax.all_to_all(sent, ('tm', 'lat'), 0, 0, tiled=True)  20.1 us
    pallas_call x1, Pallas kernels, spectra_and_contract(): pl.pallas_call(functools.partial(spectra_kernel, plan, 1.0 / math.sqrt(nl...  18.2 us
    pallas_call x1, Pallas kernels, out_tile(): pl.pallas_call(functools.partial(tile_kernel, plan), in_specs=[spot_in(pl...  4.44 us
    pallas_call x1, Pallas kernels, panel_small(): pl.pallas_call(functools.partial(panel_kernel, plan), grid=(1,), in_specs...  4.04 us
  transfers between devices with their start and end apart: 1, of which 0 were waited for; matrix products, arithmetic and copies ran while one was open for 0% of the time, Pallas kernels for 8%

profile of v7, /device:TPU:1, one launch (start us, length us, event | category | flops | bytes accessed | tf_op | source)
XLA Modules:
  0.0 48.1 jit_solution(15101236932624389936)
XLA Ops:
  1.3 18.2 %spectra_and_contract.1 = (bf16[32,16,384]{2,1,0:T(8,128)(2,1)S(1)}, f32[1,8192]{1,0:T(1,128)S(1)}) custom-call(s32[1]{0:T(128)S(6)} %copy.7.start_ref, f32[1]{0:T(128)S(6)} %copy.8.ridge_ref, s32[3,16384]{1,0:T(4,128)} %order_ref.1, bf16[2,360,1440]{2,1,0:T(8,128)(2,1)} %fields_ref.1, bf16[1440,720]{1,0:T(8,128)(2,1)} %constant.2.clone.basis_ref, ...), custom_call_target="tpu_custom_call" | custom-call | flops 12884901888 | bytes 8388608 | tf_op jit(solution)/shard_map/spectra_and_contract/pallas_call | solution.py:234
  19.5 20.1 %all_to_all.5.got_ref.own_ref = bf16[32,16,384]{2,1,0:T(8,128)(2,1)S(1)} all-to-all(bf16[32,16,384]{2,1,0:T(8,128)(2,1)S(1)} %get-tuple-element.10), channel_id=1, replica_groups=mesh['tm'=16,'lat'=2] {'tm','lat'}, dimensions={0} | all-to-all | bytes 786432 | tf_op jit(solution)/shard_map/all_to_all | solution.py:512
  39.6 0.0 collective-permute-start
  39.6 4.0 %panel_small.1 = (f32[32,512]{1,0:T(8,128)S(1)}, f32[1,512]{1,0:T(1,128)S(1)}, f32[32,128]{1,0:T(8,128)S(1)}) custom-call(bf16[32,16,384]{2,1,0:T(8,128)(2,1)S(1)} %all_to_all.5.got_ref.own_ref, f32[1,8192]{1,0:T(1,128)S(1)} %get-tuple-element.11.lam_ref), custom_call_target="tpu_custom_call" | custom-call | flops 4294967296 | bytes 262144 | tf_op jit(solution)/shard_map/panel_small/pallas_call | solution.py:333
  43.6 0.0 collective-permute-done.other_ref
  43.6 4.4 %out_tile.1 = f32[512,4096]{1,0:T(8,128)} custom-call(bf16[32,16,384]{2,1,0:T(8,128)(2,1)S(1)} %all_to_all.5.got_ref.own_ref, bf16[32,16,384]{2,1,0:T(8,128)(2,1)S(1)} %collective-permute-done.other_ref, f32[32,512]{1,0:T(8,128)S(1)} %get-tuple-element.12.w_ref, f32[1,512]{1,0:T(1,128)S(1)} %get-tuple-element.13.diag_ref, ...), custom_call_target="tpu_custom_call" | custom-call | flops 268435456 | bytes 8388608 | tf_op jit(solution)/shard_map/out_tile/pallas_call | solution.py:482
Async XLA Ops:
  39.6 4.1 %collective-permute-start = (bf16[32,16,384]{2,1,0:T(8,128)(2,1)S(1)}, bf16[32,16,384]{2,1,0:T(8,128)(2,1)S(1)}, u32[]{:S(2)}, u32[]{:S(2)}) collective-permute-start(bf16[32,16,384]{2,1,0:T(8,128)(2,1)S(1)} %all_to_all.5.got_ref.own_ref), channel_id=1, source_target_pairs={{0,2},{2,0},{4,6},{6,4},{8,10},{10,8},{12,14},{14,12},{16,18},{18,... | collective-permute-start | bytes 1179656 | tf_op jit(solution)/shard_map/ppermute | solution.py:513

commit v8 on v6

--- a/solution.py
+++ b/solution.py
@@ -120,7 +120,8 @@
                     low = source + n * LANE
                     slab_ref[row : row + 1, lanes] = sums_ref[t : t + 1, low : low + LANE]
 
-        slab_ref[...] = jnp.zeros_like(slab_ref)
+        if self.first_panel + self.panel_tiles < self.across * SUB:
+            slab_ref[...] = jnp.zeros_like(slab_ref)
         fill(self.first_panel, 0, self.panel_tiles)
         for part in range(self.lat_count):
             for core in range(2):
@@ -231,7 +232,7 @@
         functools.partial(spectra_kernel, plan, 1.0 / math.sqrt(nlon)),
         in_specs=[spot_in(pltpu.SMEM)] * 2 + [spot_in(pltpu.HBM)] * 4,
         out_specs=[spot_in(pltpu.VMEM)] * 2,
-        out_shape=[jax.ShapeDtypeStruct(plan.shape, BF16), jax.ShapeDtypeStruct((1, plan.kcoef), F32)],
+        out_shape=[pltpu.VMEM(plan.shape, BF16), jax.ShapeDtypeStruct((1, plan.kcoef), F32)],
         scratch_shapes=[
             pltpu.VMEM(order.shape, jnp.int32),
             pltpu.VMEM((entries + SUB, LANE), jnp.int32),

time: 46.5 us -> 46.5 us (level)
  no operation moved by 1% of the time
where the time goes in v8:
time: 46.5 us; the launch traced here: 45.9 us
  Pallas kernels  24.5 us (53%)
  blocking collectives  20.1 us (43%)
  between operations  1.32 us (3%)
    all_to_all x1, blocking collectives, on_device(): own = lax.all_to_all(sent, ('tm', 'lat'), 0, 0, tiled=True)  20.1 us
    pallas_call x1, Pallas kernels, spectra_and_contract(): pl.pallas_call(functools.partial(spectra_kernel, plan, 1.0 / math.sqrt(nl...  16 us
    pallas_call x1, Pallas kernels, out_tile(): pl.pallas_call(functools.partial(tile_kernel, plan), in_specs=[spot_in(pl...  4.42 us
    pallas_call x1, Pallas kernels, panel_small(): pl.pallas_call(functools.partial(panel_kernel, plan), grid=(1,), in_specs...  4.05 us
  transfers between devices with their start and end apart: 1, of which 0 were waited for; matrix products, arithmetic and copies ran while one was open for 0% of the time, Pallas kernels for 9%

profile of v8, /device:TPU:1, one launch (start us, length us, event | category | flops | bytes accessed | tf_op | source)
XLA Modules:
  0.0 45.9 jit_solution(2365802155947111508)
XLA Ops:
  1.3 16.0 %spectra_and_contract.1 = (bf16[32,16,384]{2,1,0:T(8,128)(2,1)S(1)}, f32[1,8192]{1,0:T(1,128)S(1)}) custom-call(s32[1]{0:T(128)S(6)} %copy.7.start_ref, f32[1]{0:T(128)S(6)} %copy.8.ridge_ref, s32[3,16384]{1,0:T(4,128)} %order_ref.1, bf16[2,360,1440]{2,1,0:T(8,128)(2,1)} %fields_ref.1, bf16[1440,720]{1,0:T(8,128)(2,1)} %constant.2.clone.basis_ref, ...), custom_call_target="tpu_custom_call" | custom-call | flops 12884901888 | bytes 8388608 | tf_op jit(solution)/shard_map/spectra_and_contract/pallas_call | solution.py:231
  17.3 20.1 %all_to_all.5.got_ref.own_ref = bf16[32,16,384]{2,1,0:T(8,128)(2,1)S(1)} all-to-all(bf16[32,16,384]{2,1,0:T(8,128)(2,1)S(1)} %get-tuple-element.10), channel_id=1, replica_groups=mesh['tm'=16,'lat'=2] {'tm','lat'}, dimensions={0} | all-to-all | bytes 786432 | tf_op jit(solution)/shard_map/all_to_all | solution.py:509
  37.4 0.0 collective-permute-start
  37.4 4.0 %panel_small.1 = (f32[32,512]{1,0:T(8,128)S(1)}, f32[1,512]{1,0:T(1,128)S(1)}, f32[32,128]{1,0:T(8,128)S(1)}) custom-call(bf16[32,16,384]{2,1,0:T(8,128)(2,1)S(1)} %all_to_all.5.got_ref.own_ref, f32[1,8192]{1,0:T(1,128)S(1)} %get-tuple-element.11.lam_ref), custom_call_target="tpu_custom_call" | custom-call | flops 4294967296 | bytes 262144 | tf_op jit(solution)/shard_map/panel_small/pallas_call | solution.py:330
  41.5 0.0 collective-permute-done.other_ref
  41.5 4.4 %out_tile.1 = f32[512,4096]{1,0:T(8,128)} custom-call(bf16[32,16,384]{2,1,0:T(8,128)(2,1)S(1)} %all_to_all.5.got_ref.own_ref, bf16[32,16,384]{2,1,0:T(8,128)(2,1)S(1)} %collective-permute-done.other_ref, f32[32,512]{1,0:T(8,128)S(1)} %get-tuple-element.12.w_ref, f32[1,512]{1,0:T(1,128)S(1)} %get-tuple-element.13.diag_ref, ...), custom_call_target="tpu_custom_call" | custom-call | flops 268435456 | bytes 8388608 | tf_op jit(solution)/shard_map/out_tile/pallas_call | solution.py:479
Async XLA Ops:
  37.4 4.1 %collective-permute-start = (bf16[32,16,384]{2,1,0:T(8,128)(2,1)S(1)}, bf16[32,16,384]{2,1,0:T(8,128)(2,1)S(1)}, u32[]{:S(2)}, u32[]{:S(2)}) collective-permute-start(bf16[32,16,384]{2,1,0:T(8,128)(2,1)S(1)} %all_to_all.5.got_ref.own_ref), channel_id=1, source_target_pairs={{0,2},{2,0},{4,6},{6,4},{8,10},{10,8},{12,14},{14,12},{16,18},{18,... | collective-permute-start | bytes 1179656 | tf_op jit(solution)/shard_map/ppermute | solution.py:510

commit v9 on v8

--- a/solution.py
+++ b/solution.py
@@ -287,9 +287,8 @@
     ids = lax.broadcasted_iota(jnp.int32, (PANEL, PANEL), 0)
     upto = lax.broadcasted_iota(jnp.int32, (PANEL, PANEL), 1)
     tri = jnp.where(ids < upto, 1.0, 0.0).astype(BF16)
-    prefix = 0.0
-    for piece in split(z_ref[...], 3)[::-1]:
-        prefix = prefix + jnp.dot(piece, tri, preferred_element_type=F32)
+    pieces = jnp.concatenate(split(z_ref[...], 3)[::-1], axis=1)
+    prefix = jnp.dot(pieces, jnp.concatenate([tri] * 3, axis=0), preferred_element_type=F32)
     q_ref[:, :PANEL] = prefix
     q_ref[:, PANEL:] = jnp.broadcast_to(prefix[:, PANEL - 1 :] + z_ref[:, PANEL - 1 :], (total, LANE))
     y_ref[:, :PANEL] = coef

time: 46.5 us -> 46.5 us (level)
  no operation moved by 1% of the time
where the time goes in v9:
time: 46.5 us; the launch traced here: 45.9 us
  Pallas kernels  24.5 us (53%)
  blocking collectives  20.1 us (43%)
  between operations  1.32 us (3%)
    all_to_all x1, blocking collectives, on_device(): own = lax.all_to_all(sent, ('tm', 'lat'), 0, 0, tiled=True)  20.1 us
    pallas_call x1, Pallas kernels, spectra_and_contract(): pl.pallas_call(functools.partial(spectra_kernel, plan, 1.0 / math.sqrt(nl...  16 us
    pallas_call x1, Pallas kernels, out_tile(): pl.pallas_call(functools.partial(tile_kernel, plan), in_specs=[spot_in(pl...  4.44 us
    pallas_call x1, Pallas kernels, panel_small(): pl.pallas_call(functools.partial(panel_kernel, plan), grid=(1,), in_specs...  4.05 us
  transfers between devices with their start and end apart: 1, of which 0 were waited for; matrix products, arithmetic and copies ran while one was open for 0% of the time, Pallas kernels for 9%

profile of v9, /device:TPU:1, one launch (start us, length us, event | category | flops | bytes accessed | tf_op | source)
XLA Modules:
  0.0 45.9 jit_solution(805663832375172274)
XLA Ops:
  1.3 16.0 %spectra_and_contract.1 = (bf16[32,16,384]{2,1,0:T(8,128)(2,1)S(1)}, f32[1,8192]{1,0:T(1,128)S(1)}) custom-call(s32[1]{0:T(128)S(6)} %copy.7.start_ref, f32[1]{0:T(128)S(6)} %copy.8.ridge_ref, s32[3,16384]{1,0:T(4,128)} %order_ref.1, bf16[2,360,1440]{2,1,0:T(8,128)(2,1)} %fields_ref.1, bf16[1440,720]{1,0:T(8,128)(2,1)} %constant.2.clone.basis_ref, ...), custom_call_target="tpu_custom_call" | custom-call | flops 12884901888 | bytes 8388608 | tf_op jit(solution)/shard_map/spectra_and_contract/pallas_call | solution.py:231
  17.3 20.1 %all_to_all.5.got_ref.own_ref = bf16[32,16,384]{2,1,0:T(8,128)(2,1)S(1)} all-to-all(bf16[32,16,384]{2,1,0:T(8,128)(2,1)S(1)} %get-tuple-element.10), channel_id=1, replica_groups=mesh['tm'=16,'lat'=2] {'tm','lat'}, dimensions={0} | all-to-all | bytes 786432 | tf_op jit(solution)/shard_map/all_to_all | solution.py:508
  37.4 0.0 collective-permute-start
  37.4 4.0 %panel_small.1 = (f32[32,512]{1,0:T(8,128)S(1)}, f32[1,512]{1,0:T(1,128)S(1)}, f32[32,128]{1,0:T(8,128)S(1)}) custom-call(bf16[32,16,384]{2,1,0:T(8,128)(2,1)S(1)} %all_to_all.5.got_ref.own_ref, f32[1,8192]{1,0:T(1,128)S(1)} %get-tuple-element.11.lam_ref), custom_call_target="tpu_custom_call" | custom-call | flops 4294967296 | bytes 262144 | tf_op jit(solution)/shard_map/panel_small/pallas_call | solution.py:329
  41.5 0.0 collective-permute-done.other_ref
  41.5 4.4 %out_tile.1 = f32[512,4096]{1,0:T(8,128)} custom-call(bf16[32,16,384]{2,1,0:T(8,128)(2,1)S(1)} %all_to_all.5.got_ref.own_ref, bf16[32,16,384]{2,1,0:T(8,128)(2,1)S(1)} %collective-permute-done.other_ref, f32[32,512]{1,0:T(8,128)S(1)} %get-tuple-element.12.w_ref, f32[1,512]{1,0:T(1,128)S(1)} %get-tuple-element.13.diag_ref, ...), custom_call_target="tpu_custom_call" | custom-call | flops 268435456 | bytes 8388608 | tf_op jit(solution)/shard_map/out_tile/pallas_call | solution.py:478
Async XLA Ops:
  37.4 4.1 %collective-permute-start = (bf16[32,16,384]{2,1,0:T(8,128)(2,1)S(1)}, bf16[32,16,384]{2,1,0:T(8,128)(2,1)S(1)}, u32[]{:S(2)}, u32[]{:S(2)}) collective-permute-start(bf16[32,16,384]{2,1,0:T(8,128)(2,1)S(1)} %all_to_all.5.got_ref.own_ref), channel_id=1, source_target_pairs={{0,2},{2,0},{4,6},{6,4},{8,10},{10,8},{12,14},{14,12},{16,18},{18,... | collective-permute-start | bytes 1179656 | tf_op jit(solution)/shard_map/ppermute | solution.py:509
